TPU v7x, 256 devices: a whole 4x4x8 slice. The times are simulated.
256 devices in a mesh: replica: 16 (over z_hi, x), fsdp: 8 (over y, core), tensor: 2 (over z_lo).
Axes of the slice: x: 4, y: 4, z: 8 (z_hi: 4, z_lo: 2; z = z_hi * 2 + z_lo), core: 2. Of those that a mesh axis runs over, the one named last changes fastest.
Arguments:
- activations: bfloat16 [49152, 8192], P(('replica', 'fsdp'), 'tensor'), may hold values from -6 to 6
- key_weight: bfloat16 [16, 8192, 512], P('replica', 'fsdp', 'tensor'), may hold values from -0.0625 to 0.0625
- key_cotangent: bfloat16 [49152, 512], P(('replica', 'fsdp'), 'tensor'), may hold values from -6 to 6
- outer_mantissa: bfloat16 [16, 4, 8192, 512], P('replica', None, 'fsdp', 'tensor'), may hold values from -6 to 6
- outer_exponent: int32 [16, 4, 8192, 4], P('replica', None, 'fsdp', 'tensor'), may hold values from -8 to -6
- round_index: int32 [1], replicated, may hold values from 0 to 65535
- global_weight: float32 [4, 8192, 512], P(None, ('fsdp', 'replica'), 'tensor'), may hold values from -0.0625 to 0.0625
- outer_momentum: float32 [4, 8192, 512], P(None, ('fsdp', 'replica'), 'tensor'), may hold values from -0.06 to 0.06
Outputs:
- key_states: bfloat16 [49152, 512], P(('replica', 'fsdp'), 'tensor')
- input_grad: bfloat16 [49152, 8192], P(('replica', 'fsdp'), 'tensor')
- weight_grad: bfloat16 [16, 8192, 512], P('replica', 'fsdp', 'tensor')
- global_weight_out: float32 [4, 8192, 512], P(None, ('fsdp', 'replica'), 'tensor')
- momentum_out: float32 [4, 8192, 512], P(None, ('fsdp', 'replica'), 'tensor')
- fragment_weight: bfloat16 [8192, 512], P('fsdp', 'tensor')
All inputs are finite; a program needn't handle non-finite values.
Results may differ from a plain program's by a relative error of at most 0.017.
Values may be sent and summed in bfloat16 or wider, within the bound.
A program may use at most 128 MiB of HBM per device.

v0:
```python
import jax
import jax.numpy as jnp
from jax import lax
from jax.sharding import PartitionSpec as P

BLOCK = 128


outer_rate = 0.7
outer_beta = 0.9


def local(
    activations,
    key_weight,
    key_cotangent,
    outer_mantissa,
    outer_exponent,
    round_index,
    global_weight,
    outer_momentum,
):
    gathered = lax.all_gather(activations, "tensor", axis=1, tiled=True)
    local_weight = key_weight[0]
    columns = gathered
    key_total = jnp.dot(
        columns,
        lax.all_gather(local_weight, "fsdp", axis=0, tiled=True),
        preferred_element_type=jnp.float32,
    )
    key_states = key_total.astype(jnp.bfloat16)
    input_terms = lax.dot_general(
        key_cotangent,
        lax.all_gather(local_weight, "fsdp", axis=0, tiled=True),
        (((1,), (1,)), ((), ())),
        preferred_element_type=jnp.float32,
    )
    input_grad = lax.psum_scatter(
        input_terms.astype(jnp.bfloat16), "tensor", scatter_dimension=1, tiled=True
    )
    columns = gathered
    weight_rows = lax.psum_scatter(
        lax.dot_general(
            columns, key_cotangent, (((0,), (0,)), ((), ())), preferred_element_type=jnp.float32
        ).astype(jnp.bfloat16),
        "fsdp",
        scatter_dimension=0,
        tiled=True,
    )
    weight_grad = weight_rows[None]
    fragment = jnp.remainder(round_index[0], jnp.int32(global_weight.shape[0]))
    mantissa = lax.dynamic_index_in_dim(outer_mantissa[0], fragment, 0, False).astype(jnp.float32)
    exponent = lax.dynamic_index_in_dim(outer_exponent[0], fragment, 0, False).astype(jnp.float32)
    scales = jnp.repeat(jnp.exp2(exponent), BLOCK, axis=1)
    contribution = mantissa * scales
    state_rows = global_weight.shape[1]
    summed = lax.psum(contribution.astype(jnp.bfloat16), "replica").astype(jnp.float32)
    my_share = lax.dynamic_slice_in_dim(
        summed, lax.axis_index("replica") * state_rows, state_rows, 0
    )
    delta = my_share / lax.axis_size("replica")
    old_moment = lax.dynamic_index_in_dim(outer_momentum, fragment, 0, False)
    old_weight = lax.dynamic_index_in_dim(global_weight, fragment, 0, False)
    new_moment = outer_beta * old_moment + delta
    new_weight = old_weight - outer_rate * (delta + outer_beta * new_moment)
    momentum_out = lax.dynamic_update_index_in_dim(outer_momentum, new_moment, fragment, 0)
    global_weight_out = lax.dynamic_update_index_in_dim(global_weight, new_weight, fragment, 0)
    fragment_weight = lax.all_gather(new_weight.astype(jnp.bfloat16), "replica", axis=0, tiled=True)
    return (key_states, input_grad, weight_grad, global_weight_out, momentum_out, fragment_weight)


def solution(mesh):
    placed = (
        P(("replica", "fsdp"), "tensor"),
        P("replica", "fsdp", "tensor"),
        P(("replica", "fsdp"), "tensor"),
        P("replica", None, "fsdp", "tensor"),
        P("replica", None, "fsdp", "tensor"),
        P(),
        P(None, ("fsdp", "replica"), "tensor"),
        P(None, ("fsdp", "replica"), "tensor"),
    )
    return jax.shard_map(
        local,
        mesh=mesh,
        in_specs=placed,
        out_specs=(
            P(("replica", "fsdp"), "tensor"),
            P(("replica", "fsdp"), "tensor"),
            P("replica", "fsdp", "tensor"),
            P(None, ("fsdp", "replica"), "tensor"),
            P(None, ("fsdp", "replica"), "tensor"),
            P("fsdp", "tensor"),
        ),
        check_vma=False,
    )
```

profile of v0, /device:TPU:32, one launch (start us, length us, event | category | flops | bytes accessed | tf_op | source)
XLA Modules:
  0.0 368.2 jit_solution(2402139664736052262)
XLA Ops:
  8.0 0.0 copy-start
  8.0 0.0 all-gather.4.cloned.1.call-start
  8.1 1.0 copy.24
  9.0 0.9 copy.25
  10.0 0.0 all-gather.4.cloned.1.call-update
  10.0 0.0 all-gather.6.cloned.1.call-start
  10.1 0.7 all-gather.6.cloned.1.call-update
  10.8 0.0 all-reduce.2.cloned.1.call-start
  11.5 0.7 exponential_bitcast_fusion
  12.2 0.2 copy.14
  12.4 1.2 broadcast_in_dim.14
  13.7 2.0 fusion.6
  15.6 0.0 all-reduce.2.cloned.1.call-update
  15.7 0.0 reduce-scatter.5.cloned.1.call-start
  15.7 82.2 %all-gather.4.cloned.1.call-done = bf16[384,8192]{1,0:T(8,128)(2,1)} async-done(((bf16[384,4096]{1,0:T(8,128)(2,1)}), bf16[384,8192]{1,0:T(8,128)(2,1)}) %all-gather.4.cloned.1.call-update) | async-done | bytes 6291472 | tf_op jit(solution)/shard_map/all_gather | solution.py:23
  97.9 0.0 copy-done
  97.9 7.2 %convolution_convert_fusion.1 = bf16[8192,256]{1,0:T(8,128)(2,1)} fusion(bf16[384,8192]{1,0:T(8,128)(2,1)} %all-gather.4.cloned.1.call-done, bf16[384,256]{1,0:T(8,128)(2,1)S(1)} %copy-done), kind=kOutput, calls=%fused_computation.1 | convolution fusion | flops 1612709888 | bytes 10682368 | tf_op jit(solution)/shard_map/dot_general | solution.py:43
  105.1 0.0 reduce-scatter.5.cloned.1.call-update
  105.1 0.0 reduce-scatter.3.cloned.1.call-start
  105.2 31.5 %all-gather.6.cloned.1.call-done = bf16[1,8192,256]{2,1,0:T(8,128)(2,1)} async-done(((bf16[1,1024,256]{2,1,0:T(8,128)(2,1)}), bf16[1,8192,256]{2,1,0:T(8,128)(2,1)}) %all-gather.6.cloned.1.call-update) | async-done | bytes 4194320 | tf_op jit(solution)/shard_map/all_gather | solution.py:28
  136.6 6.7 %convolution_convert_fusion = bf16[384,8192]{1,0:T(8,128)(2,1)} fusion(bf16[384,256]{1,0:T(8,128)(2,1)S(1)} %copy-done, bf16[1,8192,256]{2,1,0:T(8,128)(2,1)} %all-gather.6.cloned.1.call-done), kind=kOutput, calls=%fused_computation | convolution fusion | flops 1613758464 | bytes 10682368 | tf_op jit(solution)/shard_map/dot_general | solution.py:32
  143.3 0.0 reduce-scatter.3.cloned.1.call-update
  143.3 160.5 %all-reduce.2.cloned.1.call-done = bf16[1024,256]{1,0:T(8,128)(2,1)} async-done(((bf16[1024,256]{1,0:T(8,128)(2,1)}), bf16[1024,256]{1,0:T(8,128)(2,1)}) %all-reduce.2.cloned.1.call-update) | async-done | bytes 524304 | tf_op jit(solution)/shard_map/psum | solution.py:57
  303.8 0.8 fusion.7
  304.6 48.9 %all_gather.12 = bf16[1024,256]{1,0:T(8,128)(2,1)S(1)} all-gather(bf16[64,256]{1,0:T(8,128)(2,1)S(1)} %get-tuple-element.6), channel_id=1, replica_groups=mesh['replica'=16,'fsdp'=8,'tensor'=2] {'replica'}, dimensions={0}, use_global_device_ids=true | all-gather | bytes 557056 | tf_op jit(solution)/shard_map/all_gather | solution.py:68
  353.5 0.0 copy-start.1
  353.5 0.0 copy-start.2
  353.6 6.7 %fusion.3 = bf16[384,256]{1,0:T(8,128)(2,1)} fusion(bf16[384,8192]{1,0:T(8,128)(2,1)} %all-gather.4.cloned.1.call-done, bf16[1,8192,256]{2,1,0:T(8,128)(2,1)} %all-gather.6.cloned.1.call-done), kind=kOutput, calls=%fused_computation.5 | convolution fusion | flops 1610711040 | bytes 10682368 | tf_op jit(solution)/shard_map/dot_general | solution.py:26
  360.2 0.0 copy-done.1
  360.2 0.0 copy-done.2
  360.2 0.0 reduce-scatter.5.cloned.1.call-done
  360.2 0.0 reduce-scatter.3.cloned.1.call-done
  360.3 0.8 copy.26
  (1 shorter events, 0.0 us)
Async XLA Ops:
  8.0 89.9 %copy-start = (bf16[384,256]{1,0:T(8,128)(2,1)S(1)}, bf16[384,256]{1,0:T(8,128)(2,1)}, u32[]{:S(2)}) copy-start(bf16[384,256]{1,0:T(8,128)(2,1)} %param.10) | copy-start | bytes 589828
  8.0 89.9 %all-gather.4.cloned.1.call-start = ((), (), s32[]{:S(2)}) async-start(), calls=%async_computation.2 | async-start | bytes 9437184 | tf_op jit(solution)/shard_map/all_gather | solution.py:23
  10.0 126.6 %all-gather.6.cloned.1.call-start = ((), (), s32[]{:S(2)}) async-start(), calls=%async_computation.6 | async-start | bytes 4718592 | tf_op jit(solution)/shard_map/all_gather | solution.py:28
  10.8 293.1 %all-reduce.2.cloned.1.call-start = ((), (), s32[]{:S(2)}) async-start(), calls=%async_computation.5 | async-start | bytes 1048576 | tf_op jit(solution)/shard_map/psum | solution.py:57
  15.7 344.6 %reduce-scatter.5.cloned.1.call-start = ((), (), s32[]{:S(2)}) async-start(), calls=%async_computation.4 | async-start | bytes 4718592 | tf_op jit(solution)/shard_map/reduce_scatter | solution.py:42
  105.1 255.1 %reduce-scatter.3.cloned.1.call-start = ((), (), s32[]{:S(2)}) async-start(), calls=%async_computation.3 | async-start | bytes 9437184 | tf_op jit(solution)/shard_map/reduce_scatter | solution.py:38
  353.5 6.7 %copy-start.1 = (f32[4,64,256]{2,1,0:T(8,128)}, f32[4,64,256]{2,1,0:T(8,128)S(1)}, u32[]{:S(2)}) copy-start(f32[4,64,256]{2,1,0:T(8,128)S(1)} %get-tuple-element.20) | copy-start | bytes 786436
  353.5 6.7 %copy-start.2 = (f32[4,64,256]{2,1,0:T(8,128)}, f32[4,64,256]{2,1,0:T(8,128)S(1)}, u32[]{:S(2)}) copy-start(f32[4,64,256]{2,1,0:T(8,128)S(1)} %get-tuple-element.21) | copy-start | bytes 786436
Sparse Core Ops, SparseCore 0:
  10.6 87.2 all-gather.3
  99.8 36.7 all-gather.5
  139.7 40.3 reduce-scatter.4
  183.2 79.9 reduce-scatter.2
Sparse Core Ops, SparseCore 1:
  15.7 288.0 all-reduce.1
where the time goes:
time: 369 us; the launch traced here: 368 us
  waiting for transfers between devices  275 us (75%)
  blocking collectives  48.9 us (13%)
  matrix products  20.5 us (6%)
  between operations  15.9 us (4%)
  local copies, waits for them, and re-layouts  4.22 us (1%)
    psum x1, waiting for transfers between devices, local(): lax.psum(contribution.astype(jnp.bfloat16), 'replica').astype(jnp.float32)  161 us
    all_gather x1, waiting for transfers between devices, local(): gathered = lax.all_gather(activations, 'tensor', axis=1, tiled=True)  82.2 us
    all_gather x1, blocking collectives, local(): lax.all_gather(new_weight.astype(jnp.bfloat16), 'replica', axis=0, tiled=...  48.9 us
    all_gather x1, waiting for transfers between devices, local(): lax.all_gather(local_weight, 'fsdp', axis=0, tiled=True)  31.5 us
  transfers between devices with their start and end apart: 5, of which 3 were waited for; matrix products, arithmetic and copies ran while one was open for 7% of the time, Pallas kernels for 0%

commit v1 on v0

v1 whole, which is shorter than its diff:
```python
import functools

import jax
import jax.numpy as jnp
from jax import lax
from jax.experimental import pallas as pl
from jax.experimental.pallas import tpu as pltpu
from jax.sharding import PartitionSpec as P

MESH = pl.DeviceIdType.MESH
F32 = jnp.float32
BF16 = jnp.bfloat16

TOK = 384
ROWS = 1024
COLS = 256
HALF = 512
WIDTH = 4096
STATE = 64
FRAGS = 4
RATE = 0.7
BETA = 0.9
LOADS = ("cot", "weight", "acts", "mant", "expo", "gw", "mom")
STORES = ("key", "wg0", "wg1", "gw", "mom", "frag", "ig0", "ig1", "ig2", "ig3")


def tt_dot(a, b):
    return lax.dot_general(a, b, (((0,), (0,)), ((), ())), preferred_element_type=F32)


def nt_dot(a, b):
    return lax.dot_general(a, b, (((1,), (1,)), ((), ())), preferred_element_type=F32)


def kernel(
    acts_hbm, weight_hbm, cot_hbm, mant_hbm, expo_hbm, round_ref, gw_hbm, mom_hbm,
    key_out, ig_out, wg_out, gw_out, mom_out, frag_out,
    acts, cot, wbuf, gsend, grecv, gsum, rv, rh, zr, ig, key, key_send, key_recv, key_final, wg,
    mant, expo, contrib, xr, xsum, zrecv, frag, gw, mom,
    ld, st, wv_s, wv_r, wh_s, wh_r, rv_s, rv_r, rh_s, rh_r, bw_s, bw_r, bg_s, bg_r, z_s, z_r,
    xs_s, xs_r, zs_s, zs_r, za_s, za_r, xa_s, xa_r,
):
    r = lax.axis_index("replica")
    f = lax.axis_index("fsdp")
    t = lax.axis_index("tensor")
    zh, x = r // 4, lax.rem(r, 4)
    y, c = f // 2, lax.rem(f, 2)
    odd = lax.rem(y, 2)
    near = (y // 2) == t
    far = (y // 2) != t
    ja = jnp.where(near, odd, 1 - odd)
    jb = 1 - ja
    cols = (t, 1 - t)
    dev_h = (r, (y + 1 - 2 * odd) * 2 + c, t)
    dev_v = (r, (3 - y) * 2 + c, t)
    dev_z = (r, f, 1 - t)
    dev_s = (r, y * 2 + 1 - c, t)
    dev_x = [(zh * 4 + lax.rem(x + d, 4), f, t) for d in (1, 2, 3)]
    dev_zh = [(lax.rem(zh + d, 4) * 4 + x, f, t) for d in (1, 2, 3)]

    barrier = pltpu.get_barrier_semaphore()
    everyone = [dev_h, dev_v, dev_z, dev_s, *dev_x, *dev_zh]
    for device in everyone:
        pl.semaphore_signal(barrier, inc=1, device_id=device, device_id_type=MESH)

    def load(name, src, dst):
        return pltpu.make_async_copy(src, dst, ld.at[LOADS.index(name)])

    def store(name, src, dst):
        copy = pltpu.make_async_copy(src, dst, st.at[STORES.index(name)])
        copy.start()
        return copy

    def remote(src, dst, s, r_, i, device):
        return pltpu.make_async_remote_copy(
            src_ref=src, dst_ref=dst, send_sem=s.at[i], recv_sem=r_.at[i], device_id=device, device_id_type=MESH
        )

    load_cot = load("cot", cot_hbm, cot.at[t])
    load_weight = load("weight", weight_hbm, wbuf.at[ja, c, t])
    load_acts = load("acts", acts_hbm, acts)
    load_mant = load("mant", mant_hbm, mant)
    load_expo = load("expo", expo_hbm, expo)
    load_gw = load("gw", gw_hbm, gw)
    load_mom = load("mom", mom_hbm, mom)
    load_cot.start()

    @pl.when(near)
    def _():
        load_weight.start()

    for one in (load_acts, load_mant, load_expo, load_gw, load_mom):
        one.start()

    def piece(j, plane, k, q):
        return wbuf.at[j, plane, cols[k], pl.ds(q * HALF, HALF)]

    def w_v(i, j, k, q):
        return remote(piece(j, c, k, q), piece(j, c, k, q), wv_s, wv_r, i, dev_v)

    def w_h(i, j, k, q):
        return remote(piece(j, c, k, q), piece(j, c, k, q), wh_s, wh_r, i, dev_h)

    def w_sib(w, k, q):
        j = (ja, jb)[w]
        return remote(piece(j, c, k, q), piece(j, c, k, q), bw_s, bw_r, w * 4 + k * 2 + q, dev_s)

    def w_from_sib(w, k, q):
        j = (ja, jb)[w]
        return remote(piece(j, 1 - c, k, q), piece(j, 1 - c, k, q), bw_s, bw_r, w * 4 + k * 2 + q, dev_s)

    def w_from_z(q):
        return remote(piece(ja, c, 1, q), piece(ja, c, 1, q), z_s, z_r, 1 + q, dev_z)

    def w_to_z(q):
        return remote(
            weight_hbm.at[pl.ds(q * HALF, HALF)], wbuf.at[odd, c, t, pl.ds(q * HALF, HALF)], z_s, z_r, 1 + q, dev_z
        )

    near_v = [(ja, 0, 0), (ja, 0, 1), (ja, 1, 0), (ja, 1, 1), (jb, 0, 1)]
    far_v = [(jb, 0, 0)]
    near_h = [(ja, 0, 1), (ja, 1, 0), (ja, 1, 1)]
    near_h_in = [(jb, 0, 1), (jb, 1, 0), (jb, 1, 1)]
    far_h = [(ja, 0, 0), (ja, 1, 0), (ja, 1, 1)]
    far_h_in = [(jb, 0, 0), (jb, 1, 0), (jb, 1, 1)]

    def part(p, j):
        return gsum.at[p // 2, j, p % 2]

    def g_v(i, src):
        return remote(src, rv.at[i], rv_s, rv_r, i, dev_v)

    def g_h(i, src):
        return remote(src, rh.at[i], rh_s, rh_r, i, dev_h)

    def add_into(dst, src):
        dst[...] = (dst[...].astype(F32) + src[...].astype(F32)).astype(BF16)

    pl.semaphore_wait(barrier, len(everyone))

    load_cot.wait()
    send_cot = remote(cot.at[t], cot.at[t], z_s, z_r, 0, dev_z)
    send_cot.start()

    @pl.when(near)
    def _():
        load_weight.wait()
        w_v(0, *near_v[0]).start()
        w_h(0, *near_h[0]).start()
        w_sib(0, 0, 0).start()
        w_sib(0, 0, 1).start()

    @pl.when(far)
    def _():
        w_to_z(0).start()
        w_to_z(1).start()

    def grad_blocks(k, plane, done):
        def body(i, _):
            j, q = i // 2, lax.rem(i, 2)
            at = pl.multiple_of(j * 2 * ROWS + plane * ROWS + q * HALF, HALF)
            done(j, q, tt_dot(acts[:, pl.ds(at, HALF)], cot[cols[k]]))
            return 0

        lax.fori_loop(0, 4, body, 0)

    def grad_send(k):
        def keep(j, q, block):
            gsend[k, j, q] = block.astype(BF16)

        grad_blocks(k, 1 - c, keep)
        copy = remote(gsend.at[k], grecv.at[k], bg_s, bg_r, k, dev_s)
        copy.start()
        return copy

    def grad_sum(k):
        def keep(j, q, block):
            gsum[k, j, q] = (block + grecv[k, j, q].astype(F32)).astype(BF16)

        grad_blocks(k, c, keep)

    load_acts.wait()
    send_g0 = grad_send(0)

    load_mant.wait()
    load_expo.wait()
    fragment = lax.rem(round_ref[0], FRAGS)
    power = jnp.exp2(expo[fragment].astype(F32))
    power = jnp.transpose(jnp.concatenate([power] * 4, axis=0))
    for h in range(2):
        block = mant[fragment, :, h * 128 : (h + 1) * 128].astype(F32) * power[:, h : h + 1]
        contrib[:, :, :, h * 128 : (h + 1) * 128] = block.astype(BF16).reshape(4, 4, STATE, 128)
    x_sends = [
        remote(contrib.at[:, lax.rem(x + d, 4)], xr.at[d - 1], xs_s, xs_r, d - 1, dev_x[d - 1]) for d in (1, 2, 3)
    ]
    for copy in x_sends:
        copy.start()

    send_g0.wait_recv()
    grad_sum(0)

    @pl.when(near)
    def _():
        g_h(1, part(1, jb)).start()
        w_v(1, *near_v[1]).start()

    @pl.when(far)
    def _():
        g_v(0, part(0, jb)).start()
        g_v(1, part(0, ja)).start()
        g_h(0, part(1, jb)).start()

    remote(cot.at[1 - t], cot.at[1 - t], z_s, z_r, 0, dev_z).wait_recv()
    send_g1 = grad_send(1)
    send_g1.wait_recv()
    grad_sum(1)

    @pl.when(near)
    def _():
        g_v(0, part(3, jb)).start()
        w_from_z(0).wait_recv()
        w_h(1, *near_h[1]).start()
        w_v(2, *near_v[2]).start()
        w_sib(0, 1, 0).start()
        w_from_z(1).wait_recv()
        w_h(2, *near_h[2]).start()
        w_v(3, *near_v[3]).start()
        w_sib(0, 1, 1).start()
        w_h(0, *near_h_in[0]).wait_recv()
        w_v(4, *near_v[4]).start()
        w_sib(1, 0, 1).start()
        g_h(2, part(2, jb)).start()
        g_v(0, rv.at[0]).wait_recv()
        add_into(rv.at[0], part(0, jb))
        g_h(0, rv.at[0]).start()

    @pl.when(far)
    def _():
        w_v(0, *near_v[0]).wait_recv()
        w_h(0, *far_h[0]).start()
        w_sib(0, 0, 0).start()
        g_h(1, part(2, jb)).start()
        w_h(0, *far_h_in[0]).wait_recv()
        w_v(0, *far_v[0]).start()
        w_sib(1, 0, 0).start()
        g_v(0, rv.at[0]).wait_recv()
        add_into(rv.at[0], part(3, jb))
        g_h(2, rv.at[0]).start()
        g_h(1, rh.at[1]).wait_recv()
        add_into(rh.at[1], part(2, ja))
        g_v(3, rh.at[1]).start()

    for copy in x_sends:
        copy.wait_recv()
    for i in range(4):
        total = contrib[i, x].astype(F32)
        for d in range(3):
            total = total + xr[d, i].astype(F32)
        xsum[i] = total.astype(BF16)
    z_sends = [
        remote(xsum.at[lax.rem(zh + d, 4)], zrecv.at[d - 1], zs_s, zs_r, d - 1, dev_zh[d - 1]) for d in (1, 2, 3)
    ]
    for copy in z_sends:
        copy.start()

    @pl.when(near)
    def _():
        w_h(1, *near_h_in[1]).wait_recv()
        w_sib(1, 1, 0).start()
        w_v(0, *far_v[0]).wait_recv()
        w_sib(1, 0, 0).start()
        w_h(2, *near_h_in[2]).wait_recv()
        w_sib(1, 1, 1).start()

    @pl.when(far)
    def _():
        w_v(1, *near_v[1]).wait_recv()
        w_sib(0, 0, 1).start()
        w_v(2, *near_v[2]).wait_recv()
        w_h(1, *far_h[1]).start()
        w_sib(0, 1, 0).start()
        g_h(2, rh.at[2]).wait_recv()
        add_into(rh.at[2], part(3, ja))
        g_v(4, rh.at[2]).start()
        g_h(0, rh.at[0]).wait_recv()
        add_into(rh.at[0], part(1, ja))
        g_v(2, rh.at[0]).start()

    load_gw.wait()
    load_mom.wait()
    for copy in z_sends:
        copy.wait_recv()
    total = xsum[zh].astype(F32)
    for d in range(3):
        total = total + zrecv[d].astype(F32)
    delta = total * (1.0 / 16)
    new_moment = BETA * mom[fragment] + delta
    new_weight = gw[fragment] - RATE * (delta + BETA * new_moment)
    for i in range(FRAGS):
        chosen = fragment == i
        mom[i] = jnp.where(chosen, new_moment, mom[i])
        gw[i] = jnp.where(chosen, new_weight, gw[i])
    frag[zh, x] = new_weight.astype(BF16)
    stores = [store("gw", gw, gw_out), store("mom", mom, mom_out)]
    za_sends = [remote(frag.at[zh, x], frag.at[zh, x], za_s, za_r, d - 1, dev_zh[d - 1]) for d in (1, 2, 3)]
    for copy in za_sends:
        copy.start()

    @pl.when(far)
    def _():
        w_v(3, *near_v[3]).wait_recv()
        w_h(2, *far_h[2]).start()
        w_sib(0, 1, 1).start()

    for d in (1, 2, 3):
        there = frag.at[lax.rem(zh + 4 - d, 4), x]
        remote(there, there, za_s, za_r, d - 1, dev_zh[d - 1]).wait_recv()
    xa_sends = [remote(frag.at[:, x], frag.at[:, x], xa_s, xa_r, d - 1, dev_x[d - 1]) for d in (1, 2, 3)]
    for copy in xa_sends:
        copy.start()

    key[...] = jnp.zeros_like(key)

    def block(w, plane):
        j = (ja, jb)[w]
        at = j * 2 * ROWS + plane * ROWS
        wide = pl.ds(pl.multiple_of(at, ROWS), ROWS)
        for k in range(2):
            key[k] += jnp.dot(acts[:, wide], wbuf[j, plane, cols[k]], preferred_element_type=F32)

        def body(i, _):
            rows = pl.ds(pl.multiple_of(i * COLS, COLS), COLS)
            total = nt_dot(cot[0], wbuf[j, plane, 0, rows]) + nt_dot(cot[1], wbuf[j, plane, 1, rows])
            ig[:, pl.ds(pl.multiple_of(at + i * COLS, COLS), COLS)] = total.astype(BF16)
            return 0

        lax.fori_loop(0, ROWS // COLS, body, 0)
        i = ("ig0", "ig1", "ig2", "ig3")[w * 2 + (0 if plane is c else 1)]
        return store(i, ig.at[:, wide], ig_out.at[:, wide])

    stores.append(block(0, c))
    for k in range(2):
        for q in range(2):
            w_from_sib(0, k, q).wait_recv()
    other = 1 - c
    stores.append(block(0, other))

    @pl.when(near)
    def _():
        g_v(3, rv.at[3]).wait_recv()
        g_h(2, rh.at[2]).wait_recv()
        add_into(rv.at[3], rh.at[2])
        add_into(rv.at[3], part(2, ja))
        remote(rv.at[3], zr.at[0], z_s, z_r, 4, dev_z).start()

    @pl.when(far)
    def _():
        w_v(4, *near_v[4]).wait_recv()
        w_sib(1, 0, 1).start()
        w_h(1, *far_h_in[1]).wait_recv()
        w_sib(1, 1, 0).start()
        w_h(2, *far_h_in[2]).wait_recv()
        w_sib(1, 1, 1).start()

    stores.append(block(1, c))
    for k in range(2):
        for q in range(2):
            w_from_sib(1, k, q).wait_recv()
    stores.append(block(1, other))

    key_send[...] = key[1].astype(BF16)
    send_key = remote(key_send, key_recv, z_s, z_r, 3, dev_z)
    send_key.start()

    @pl.when(near)
    def _():
        g_v(4, rv.at[4]).wait_recv()
        add_into(rv.at[4], part(3, ja))
        remote(rv.at[4], zr.at[1], z_s, z_r, 5, dev_z).start()
        g_v(1, rv.at[1]).wait_recv()
        g_h(0, rh.at[0]).wait_recv()
        total = rv[1].astype(F32) + rh[0].astype(F32) + gsum[0, ja, 0].astype(F32)
        wg[0] = total.astype(BF16)
        g_v(2, rv.at[2]).wait_recv()
        g_h(1, rh.at[1]).wait_recv()
        total = rv[2].astype(F32) + rh[1].astype(F32) + gsum[0, ja, 1].astype(F32)
        wg[1] = total.astype(BF16)
        store("wg0", wg.at[0], wg_out.at[0])
        store("wg1", wg.at[1], wg_out.at[1])

    @pl.when(far)
    def _():
        for q in range(2):
            remote(zr.at[q], zr.at[q], z_s, z_r, 4 + q, dev_z).wait_recv()
            store(f"wg{q}", zr.at[q], wg_out.at[q])

    for d in (1, 2, 3):
        there = frag.at[:, lax.rem(x + 4 - d, 4)]
        remote(there, there, xa_s, xa_r, d - 1, dev_x[d - 1]).wait_recv()
    stores.append(store("frag", frag, frag_out))

    send_key.wait_recv()
    key_final[...] = (key[0] + key_recv[...].astype(F32)).astype(BF16)
    stores.append(store("key", key_final, key_out))

    for copy in (send_cot, send_key, send_g0, send_g1, *x_sends, *z_sends, *za_sends, *xa_sends):
        copy.wait_send()
    for w in range(2):
        for k in range(2):
            for q in range(2):
                w_sib(w, k, q).wait_send()
    for i in range(3):
        g_h(i, rh.at[i]).wait_send()

    @pl.when(near)
    def _():
        for i in range(5):
            w_v(i, *near_v[i]).wait_send()
        for i in range(3):
            w_h(i, *near_h[i]).wait_send()
        g_v(0, rv.at[0]).wait_send()
        for q in range(2):
            remote(rv.at[3 + q], zr.at[q], z_s, z_r, 4 + q, dev_z).wait_send()
        for q in range(2):
            pltpu.make_async_copy(wg.at[q], wg_out.at[q], st.at[STORES.index(f"wg{q}")]).wait()

    @pl.when(far)
    def _():
        w_v(0, *far_v[0]).wait_send()
        for i in range(3):
            w_h(i, *far_h[i]).wait_send()
        for i in range(5):
            g_v(i, rv.at[i]).wait_send()
        for q in range(2):
            w_to_z(q).wait_send()
        for q in range(2):
            pltpu.make_async_copy(zr.at[q], wg_out.at[q], st.at[STORES.index(f"wg{q}")]).wait()

    for copy in stores:
        copy.wait()


def local(
    activations, key_weight, key_cotangent, outer_mantissa, outer_exponent, round_index, global_weight, outer_momentum
):
    vmem = pltpu.VMEM
    dma = lambda n: pltpu.SemaphoreType.DMA((n,))
    exponent = jnp.transpose(outer_exponent[0], (0, 2, 1))
    anywhere = pl.BlockSpec(memory_space=pl.ANY)
    outs = pl.pallas_call(
        kernel,
        out_shape=(
            jax.ShapeDtypeStruct((TOK, COLS), BF16),
            jax.ShapeDtypeStruct((TOK, WIDTH), BF16),
            jax.ShapeDtypeStruct((2, HALF, COLS), BF16),
            jax.ShapeDtypeStruct((FRAGS, STATE, COLS), F32),
            jax.ShapeDtypeStruct((FRAGS, STATE, COLS), F32),
            jax.ShapeDtypeStruct((4, 4, STATE, COLS), BF16),
        ),
        in_specs=[anywhere] * 5 + [pl.BlockSpec(memory_space=pltpu.SMEM)] + [anywhere] * 2,
        out_specs=[anywhere] * 6,
        scratch_shapes=[
            vmem((TOK, WIDTH), BF16),
            vmem((2, TOK, COLS), BF16),
            vmem((2, 2, 2, ROWS, COLS), BF16),
            vmem((2, 2, 2, HALF, COLS), BF16),
            vmem((2, 2, 2, HALF, COLS), BF16),
            vmem((2, 2, 2, HALF, COLS), BF16),
            vmem((5, HALF, COLS), BF16),
            vmem((3, HALF, COLS), BF16),
            vmem((2, HALF, COLS), BF16),
            vmem((TOK, WIDTH), BF16),
            vmem((2, TOK, COLS), F32),
            vmem((TOK, COLS), BF16),
            vmem((TOK, COLS), BF16),
            vmem((TOK, COLS), BF16),
            vmem((2, HALF, COLS), BF16),
            vmem((FRAGS, ROWS, COLS), BF16),
            vmem((FRAGS, 2, ROWS), jnp.int32),
            vmem((4, 4, STATE, COLS), BF16),
            vmem((3, 4, STATE, COLS), BF16),
            vmem((4, STATE, COLS), BF16),
            vmem((3, STATE, COLS), BF16),
            vmem((4, 4, STATE, COLS), BF16),
            vmem((FRAGS, STATE, COLS), F32),
            vmem((FRAGS, STATE, COLS), F32),
            dma(len(LOADS)), dma(len(STORES)),
            dma(5), dma(5), dma(3), dma(3), dma(5), dma(5), dma(3), dma(3),
            dma(8), dma(8), dma(2), dma(2), dma(6), dma(6),
            dma(3), dma(3), dma(3), dma(3), dma(3), dma(3), dma(3), dma(3),
        ],
        compiler_params=pltpu.CompilerParams(
            collective_id=0, has_side_effects=True, vmem_limit_bytes=44 * 2**20
        ),
    )(
        activations, key_weight[0], key_cotangent, outer_mantissa[0], exponent, round_index, global_weight,
        outer_momentum,
    )
    key_states, input_grad, weight_grad, global_weight_out, momentum_out, fragment_weight = outs
    return (
        key_states,
        input_grad,
        weight_grad.reshape(1, ROWS, COLS),
        global_weight_out,
        momentum_out,
        fragment_weight.reshape(ROWS, COLS),
    )


def solution(mesh):
    placed = (
        P(("replica", "fsdp"), "tensor"),
        P("replica", "fsdp", "tensor"),
        P(("replica", "fsdp"), "tensor"),
        P("replica", None, "fsdp", "tensor"),
        P("replica", None, "fsdp", "tensor"),
        P(),
        P(None, ("fsdp", "replica"), "tensor"),
        P(None, ("fsdp", "replica"), "tensor"),
    )
    return jax.shard_map(
        local,
        mesh=mesh,
        in_specs=placed,
        out_specs=(
            P(("replica", "fsdp"), "tensor"),
            P(("replica", "fsdp"), "tensor"),
            P("replica", "fsdp", "tensor"),
            P(None, ("fsdp", "replica"), "tensor"),
            P(None, ("fsdp", "replica"), "tensor"),
            P("fsdp", "tensor"),
        ),
        check_vma=False,
    )
```

time: 369 us -> 74.1 us (0.20)
  waiting for transfers between devices: 275 us -> 0 us
  Pallas kernels: 0 us -> 60.9 us
  blocking collectives: 48.9 us -> 0 us
  matrix products: 20.5 us -> 0 us
  between operations: 15.9 us -> 1.3 us
  local copies, waits for them, and re-layouts: 4.22 us -> 11.5 us
    psum x1 -> x0, waiting for transfers between devices: 161 us -> none  [local(): lax.psum(contribution.astype(jnp.bfloat16), 'replica').astype(jnp.float32)]
    all_gather x2 -> x0, waiting for transfers between devices: 114 us -> none  [the longest x1 82.2 us: local(): gathered = lax.all_gather(activations, 'tensor', axis=1, tiled=True)]
    pallas_call x0 -> x1, Pallas kernels: none -> 60.9 us  [local(): pl.pallas_call(kernel, out_shape=(jax.ShapeDtypeStruct((TOK, COLS), BF16)...]
    all_gather x1 -> x0, blocking collectives: 48.9 us -> none  [local(): lax.all_gather(new_weight.astype(jnp.bfloat16), 'replica', axis=0, tiled=...]
    dot_general x3 -> x0, matrix products: 20.5 us -> none  [the longest x1 7.15 us: local(): lax.dot_general(columns, key_cotangent, (((0,), (0,)), ((), ())), preferr...]
    unnamed x9 -> x18, local copies, waits for them, and re-layouts: 2.76 us -> 11.5 us
  transfers between devices with their start and end apart: 5 -> 0, of which waited for: 3 -> 0; matrix products, arithmetic and copies ran while one was open for 7% -> 0% of each run, Pallas kernels for 0% -> 0%
where the time goes in v1:
time: 74.1 us; the launch traced here: 73.8 us
  Pallas kernels  60.9 us (82%)
  local copies, waits for them, and re-layouts  11.5 us (16%)
  between operations  1.3 us (2%)
    pallas_call x1, Pallas kernels, local(): pl.pallas_call(kernel, out_shape=(jax.ShapeDtypeStruct((TOK, COLS), BF16)...  60.9 us
    unnamed x18, local copies, waits for them, and re-layouts  11.5 us

profile of v1, /device:TPU:32, one launch (start us, length us, event | category | flops | bytes accessed | tf_op | source)
XLA Modules:
  0.0 73.8 jit_solution(9353647459517462702)
XLA Ops:
  1.3 0.0 copy-start
  1.3 1.6 %copy-done = bf16[1,4,1024,256]{3,2,1,0:T(8,128)(2,1)S(1)} copy-done((bf16[1,4,1024,256]{3,2,1,0:T(8,128)(2,1)S(1)}, bf16[1,4,1024,256]{3,2,1,0:T(8,128)(2,1)}, u32[]{:S(2)}) %copy-start) | copy-done | bytes 2097176
  2.9 0.0 copy-start.1
  2.9 1.0 %copy-done.1 = bf16[1,1024,256]{2,1,0:T(8,128)(2,1)S(1)} copy-done((bf16[1,1024,256]{2,1,0:T(8,128)(2,1)S(1)}, bf16[1,1024,256]{2,1,0:T(8,128)(2,1)}, u32[]{:S(2)}) %copy-start.1) | copy-done | bytes 524312
  3.9 0.0 copy-start.2
  3.9 0.9 %copy-done.2 = f32[4,64,256]{2,1,0:T(8,128)S(1)} copy-done((f32[4,64,256]{2,1,0:T(8,128)S(1)}, f32[4,64,256]{2,1,0:T(8,128)}, u32[]{:S(2)}) %copy-start.2) | copy-done | bytes 262168
  4.9 0.0 copy-start.3
  4.9 0.9 %copy-done.3 = f32[4,64,256]{2,1,0:T(8,128)S(1)} copy-done((f32[4,64,256]{2,1,0:T(8,128)S(1)}, f32[4,64,256]{2,1,0:T(8,128)}, u32[]{:S(2)}) %copy-start.3) | copy-done | bytes 262168
  5.8 0.0 copy-start.4
  5.8 0.9 %copy-done.4 = bf16[384,256]{1,0:T(8,128)(2,1)S(1)} copy-done((bf16[384,256]{1,0:T(8,128)(2,1)S(1)}, bf16[384,256]{1,0:T(8,128)(2,1)}, u32[]{:S(2)}) %copy-start.4) | copy-done | bytes 196632
  6.7 0.0 copy-start.5
  6.7 0.8 %copy-done.5 = s32[1,4,1024,2]{2,3,1,0:T(2,128)S(1)} copy-done((s32[1,4,1024,2]{2,3,1,0:T(2,128)S(1)}, s32[1,4,1024,2]{2,3,1,0:T(2,128)}, u32[]{:S(2)}) %copy-start.5) | copy-done | bytes 32792
  7.5 60.9 %shard_map.127 = (bf16[384,256]{1,0:T(8,128)(2,1)S(1)}, bf16[384,4096]{1,0:T(8,128)(2,1)S(1)}, bf16[2,512,256]{2,1,0:T(8,128)(2,1)S(1)}, f32[4,64,256]{2,1,0:T(8...) custom-call(bf16[384,4096]{1,0:T(8,128)(2,1)} %acts_hbm.1, bf16[1024,256]{1,0:T(8,128)(2,1)S(1)} %bitcast.8, ...), custom_call_target="tpu_custom_call" | custom-call | tf_op jit(solution)/shard_map/pallas_call | solution.py:450
  68.4 0.7 copy.21
  69.1 1.7 %copy.22 = bf16[384,4096]{1,0:T(8,128)(2,1)} copy(bf16[384,4096]{1,0:T(8,128)(2,1)S(1)} %get-tuple-element.25) | data formatting | bytes 6291456
  70.8 0.8 %copy.23 = bf16[1,1024,256]{2,1,0:T(8,128)(2,1)} copy(bf16[1,1024,256]{2,1,0:T(8,128)(2,1)S(1)} %bitcast.10) | data formatting | bytes 1048576
  71.6 0.7 copy.24
  72.3 0.7 copy.25
  73.0 0.8 %copy.26 = bf16[1024,256]{1,0:T(8,128)(2,1)} copy(bf16[1024,256]{1,0:T(8,128)(2,1)S(1)} %bitcast.9) | data formatting | bytes 1048576
Async XLA Ops:
  1.3 1.6 %copy-start = (bf16[1,4,1024,256]{3,2,1,0:T(8,128)(2,1)S(1)}, bf16[1,4,1024,256]{3,2,1,0:T(8,128)(2,1)}, u32[]{:S(2)}) copy-start(bf16[1,4,1024,256]{3,2,1,0:T(8,128)(2,1)} %param.11) | copy-start | bytes 6291460
  2.9 1.0 %copy-start.1 = (bf16[1,1024,256]{2,1,0:T(8,128)(2,1)S(1)}, bf16[1,1024,256]{2,1,0:T(8,128)(2,1)}, u32[]{:S(2)}) copy-start(bf16[1,1024,256]{2,1,0:T(8,128)(2,1)} %param.9) | copy-start | bytes 1572868
  3.9 0.9 %copy-start.2 = (f32[4,64,256]{2,1,0:T(8,128)S(1)}, f32[4,64,256]{2,1,0:T(8,128)}, u32[]{:S(2)}) copy-start(f32[4,64,256]{2,1,0:T(8,128)} %gw_hbm.1) | copy-start | bytes 786436
  4.9 0.9 %copy-start.3 = (f32[4,64,256]{2,1,0:T(8,128)S(1)}, f32[4,64,256]{2,1,0:T(8,128)}, u32[]{:S(2)}) copy-start(f32[4,64,256]{2,1,0:T(8,128)} %mom_hbm.1) | copy-start | bytes 786436
  5.8 0.9 %copy-start.4 = (bf16[384,256]{1,0:T(8,128)(2,1)S(1)}, bf16[384,256]{1,0:T(8,128)(2,1)}, u32[]{:S(2)}) copy-start(bf16[384,256]{1,0:T(8,128)(2,1)} %cot_hbm.1) | copy-start | bytes 589828
  6.7 0.8 %copy-start.5 = (s32[1,4,1024,2]{2,3,1,0:T(2,128)S(1)}, s32[1,4,1024,2]{2,3,1,0:T(2,128)}, u32[]{:S(2)}) copy-start(s32[1,4,1024,2]{2,3,1,0:T(2,128)} %param.12) | copy-start | bytes 98308

commit v2 on v1

v2 whole, which is shorter than its diff:
```python
import functools

import jax
import jax.numpy as jnp
from jax import lax
from jax.experimental import pallas as pl
from jax.experimental.pallas import tpu as pltpu
from jax.sharding import PartitionSpec as P

MESH = pl.DeviceIdType.MESH
F32 = jnp.float32
BF16 = jnp.bfloat16

TOK = 384
ROWS = 1024
COLS = 256
HALF = 512
WIDTH = 4096
STATE = 64
FRAGS = 4
RATE = 0.7
BETA = 0.9
LOADS = ("cot", "weight", "acts", "mant", "expo", "gw", "mom")


def tt_dot(a, b):
    return lax.dot_general(a, b, (((0,), (0,)), ((), ())), preferred_element_type=F32)


def nt_dot(a, b):
    return lax.dot_general(a, b, (((1,), (1,)), ((), ())), preferred_element_type=F32)


def kernel(
    acts_hbm, weight_hbm, cot_hbm, mant_hbm, expo_hbm, round_ref, gw_hbm, mom_hbm,
    key_out, ig_out, wg_out, gw_out, mom_out, frag_out,
    acts, cot, wbuf, gsend, grecv, gsum, rv, rh, zr, key, key_send, key_recv,
    mant, expo, contrib, xr, xsum, zrecv, frag, gw, mom,
    ld, wv_s, wv_r, wh_s, wh_r, rv_s, rv_r, rh_s, rh_r, bw_s, bw_r, bg_s, bg_r, z_s, z_r,
    xs_s, xs_r, zs_s, zs_r, za_s, za_r, xa_s, xa_r,
):
    r = lax.axis_index("replica")
    f = lax.axis_index("fsdp")
    t = lax.axis_index("tensor")
    zh, x = r // 4, lax.rem(r, 4)
    y, c = f // 2, lax.rem(f, 2)
    odd = lax.rem(y, 2)
    near = (y // 2) == t
    far = (y // 2) != t
    ja = jnp.where(near, odd, 1 - odd)
    jb = 1 - ja
    cols = (t, 1 - t)
    dev_h = (r, (y + 1 - 2 * odd) * 2 + c, t)
    dev_v = (r, (3 - y) * 2 + c, t)
    dev_z = (r, f, 1 - t)
    dev_s = (r, y * 2 + 1 - c, t)
    dev_x = [(zh * 4 + lax.rem(x + d, 4), f, t) for d in (1, 2, 3)]
    dev_zh = [(lax.rem(zh + d, 4) * 4 + x, f, t) for d in (1, 2, 3)]

    barrier = pltpu.get_barrier_semaphore()
    everyone = [dev_h, dev_v, dev_z, dev_s, *dev_x, *dev_zh]
    for device in everyone:
        pl.semaphore_signal(barrier, inc=1, device_id=device, device_id_type=MESH)

    def load(name, src, dst):
        return pltpu.make_async_copy(src, dst, ld.at[LOADS.index(name)])

    def remote(src, dst, s, r_, i, device):
        return pltpu.make_async_remote_copy(
            src_ref=src, dst_ref=dst, send_sem=s.at[i], recv_sem=r_.at[i], device_id=device, device_id_type=MESH
        )

    load_cot = load("cot", cot_hbm, cot.at[t])
    load_weight = load("weight", weight_hbm, wbuf.at[ja, c, t])
    load_acts = load("acts", acts_hbm, acts)
    load_mant = load("mant", mant_hbm, mant)
    load_expo = load("expo", expo_hbm, expo)
    load_gw = load("gw", gw_hbm, gw)
    load_mom = load("mom", mom_hbm, mom)
    load_cot.start()

    @pl.when(near)
    def _():
        load_weight.start()

    for one in (load_acts, load_mant, load_expo, load_gw, load_mom):
        one.start()

    def piece(j, plane, k, q):
        return wbuf.at[j, plane, cols[k], pl.ds(q * HALF, HALF)]

    def w_v(i, j, k, q):
        return remote(piece(j, c, k, q), piece(j, c, k, q), wv_s, wv_r, i, dev_v)

    def w_h(i, j, k, q):
        return remote(piece(j, c, k, q), piece(j, c, k, q), wh_s, wh_r, i, dev_h)

    def w_sib(w, k, q):
        j = (ja, jb)[w]
        return remote(piece(j, c, k, q), piece(j, c, k, q), bw_s, bw_r, w * 4 + k * 2 + q, dev_s)

    def w_from_sib(w, k, q):
        j = (ja, jb)[w]
        return remote(piece(j, 1 - c, k, q), piece(j, 1 - c, k, q), bw_s, bw_r, w * 4 + k * 2 + q, dev_s)

    def w_from_z(q):
        return remote(piece(ja, c, 1, q), piece(ja, c, 1, q), z_s, z_r, 1 + q, dev_z)

    def w_to_z(q):
        return remote(
            weight_hbm.at[pl.ds(q * HALF, HALF)], wbuf.at[odd, c, t, pl.ds(q * HALF, HALF)], z_s, z_r, 1 + q, dev_z
        )

    near_v = [(ja, 0, 0), (ja, 1, 0), (ja, 1, 1), (ja, 0, 1), (jb, 0, 1)]
    far_v = [(jb, 0, 0)]
    near_h = [(ja, 0, 1), (ja, 1, 0), (ja, 1, 1)]
    near_h_in = [(jb, 0, 1), (jb, 1, 0), (jb, 1, 1)]
    far_h = [(ja, 0, 0), (ja, 1, 0), (ja, 1, 1)]
    far_h_in = [(jb, 0, 0), (jb, 1, 0), (jb, 1, 1)]

    def part(p, w):
        return gsum.at[p // 2, w, p % 2]

    def g_v(i, src):
        return remote(src, rv.at[i], rv_s, rv_r, i, dev_v)

    def g_h(i, src):
        return remote(src, rh.at[i], rh_s, rh_r, i, dev_h)

    def add_into(dst, src):
        dst[...] = (dst[...].astype(F32) + src[...].astype(F32)).astype(BF16)

    pl.semaphore_wait(barrier, len(everyone))

    send_cot = remote(cot.at[t], cot.at[t], z_s, z_r, 0, dev_z)

    @pl.when(near)
    def _():
        load_weight.wait()
        w_v(0, *near_v[0]).start()
        w_h(0, *near_h[0]).start()
        w_sib(0, 0, 0).start()
        w_sib(0, 0, 1).start()

    @pl.when(far)
    def _():
        w_to_z(0).start()

    load_cot.wait()
    send_cot.start()

    @pl.when(far)
    def _():
        w_to_z(1).start()

    def grad_block(k, w, plane, q):
        at = (ja, jb)[w] * 2 * ROWS + plane * ROWS + q * HALF
        return tt_dot(acts[:, pl.ds(pl.multiple_of(at, HALF), HALF)], cot[cols[k]])

    def grad_send(k, q):
        for w in range(2):
            gsend[k, q, w] = grad_block(k, w, 1 - c, q).astype(BF16)
        copy = remote(gsend.at[k, q], grecv.at[k, q], bg_s, bg_r, k * 2 + q, dev_s)
        copy.start()
        return copy

    def grad_sum(k, q, copy):
        copy.wait_recv()
        for w in range(2):
            gsum[k, w, q] = (grad_block(k, w, c, q) + grecv[k, q, w].astype(F32)).astype(BF16)

    load_acts.wait()
    send_g = {}
    for q in range(2):
        send_g[0, q] = grad_send(0, q)
    grad_sum(0, 0, send_g[0, 0])

    @pl.when(far)
    def _():
        g_v(0, part(0, 1)).start()
        g_v(1, part(0, 0)).start()

    grad_sum(0, 1, send_g[0, 1])

    @pl.when(near)
    def _():
        g_h(1, part(1, 1)).start()

    @pl.when(far)
    def _():
        g_h(0, part(1, 1)).start()

    load_mant.wait()
    load_expo.wait()
    fragment = lax.rem(round_ref[0], FRAGS)
    power = jnp.exp2(expo[fragment].astype(F32))
    power = jnp.transpose(jnp.concatenate([power] * 4, axis=0))
    for h in range(2):
        block = mant[fragment, :, h * 128 : (h + 1) * 128].astype(F32) * power[:, h : h + 1]
        contrib[:, :, :, h * 128 : (h + 1) * 128] = block.astype(BF16).reshape(4, 4, STATE, 128)
    x_sends = [
        remote(contrib.at[:, lax.rem(x + d, 4)], xr.at[d - 1], xs_s, xs_r, d - 1, dev_x[d - 1]) for d in (1, 2, 3)
    ]
    for copy in x_sends:
        copy.start()

    @pl.when(near)
    def _():
        w_from_z(0).wait_recv()
        w_v(1, *near_v[1]).start()
        w_h(1, *near_h[1]).start()
        w_sib(0, 1, 0).start()
        w_h(0, *near_h_in[0]).wait_recv()
        w_sib(1, 0, 1).start()

    @pl.when(far)
    def _():
        w_v(0, *near_v[0]).wait_recv()
        w_h(0, *far_h[0]).start()
        w_sib(0, 0, 0).start()

    remote(cot.at[1 - t], cot.at[1 - t], z_s, z_r, 0, dev_z).wait_recv()
    for q in (1, 0):
        send_g[1, q] = grad_send(1, q)
    grad_sum(1, 1, send_g[1, 1])

    @pl.when(near)
    def _():
        g_v(0, part(3, 1)).start()

    grad_sum(1, 0, send_g[1, 0])

    @pl.when(near)
    def _():
        g_h(2, part(2, 1)).start()

    @pl.when(far)
    def _():
        g_h(1, part(2, 1)).start()

    for copy in x_sends:
        copy.wait_recv()
    for i in range(4):
        total = contrib[i, x].astype(F32)
        for d in range(3):
            total = total + xr[d, i].astype(F32)
        xsum[i] = total.astype(BF16)
    z_sends = [
        remote(xsum.at[lax.rem(zh + d, 4)], zrecv.at[d - 1], zs_s, zs_r, d - 1, dev_zh[d - 1]) for d in (1, 2, 3)
    ]
    for copy in z_sends:
        copy.start()

    @pl.when(near)
    def _():
        w_from_z(1).wait_recv()
        w_v(2, *near_v[2]).start()
        w_h(2, *near_h[2]).start()
        w_v(3, *near_v[3]).start()
        w_v(4, *near_v[4]).start()
        w_sib(0, 1, 1).start()
        w_h(1, *near_h_in[1]).wait_recv()
        w_sib(1, 1, 0).start()
        g_v(0, rv.at[0]).wait_recv()
        add_into(rv.at[0], part(0, 1))
        g_h(0, rv.at[0]).start()

    @pl.when(far)
    def _():
        w_h(0, *far_h_in[0]).wait_recv()
        w_v(0, *far_v[0]).start()
        w_sib(1, 0, 0).start()
        w_v(1, *near_v[1]).wait_recv()
        w_sib(0, 1, 0).start()
        g_v(0, rv.at[0]).wait_recv()
        add_into(rv.at[0], part(3, 1))
        g_h(2, rv.at[0]).start()
        g_h(1, rh.at[1]).wait_recv()
        add_into(rh.at[1], part(2, 0))
        g_v(3, rh.at[1]).start()

    load_gw.wait()
    load_mom.wait()
    for copy in z_sends:
        copy.wait_recv()
    total = xsum[zh].astype(F32)
    for d in range(3):
        total = total + zrecv[d].astype(F32)
    delta = total * (1.0 / 16)
    new_moment = BETA * mom[fragment] + delta
    new_weight = gw[fragment] - RATE * (delta + BETA * new_moment)
    for i in range(FRAGS):
        chosen = fragment == i
        mom_out[i] = jnp.where(chosen, new_moment, mom[i])
        gw_out[i] = jnp.where(chosen, new_weight, gw[i])
    frag[zh, x] = new_weight.astype(BF16)
    za_sends = [remote(frag.at[zh, x], frag.at[zh, x], za_s, za_r, d - 1, dev_zh[d - 1]) for d in (1, 2, 3)]
    for copy in za_sends:
        copy.start()

    @pl.when(far)
    def _():
        w_v(2, *near_v[2]).wait_recv()
        w_h(2, *far_h[2]).start()
        w_h(1, *far_h[1]).start()
        w_sib(0, 1, 1).start()
        g_h(2, rh.at[2]).wait_recv()
        add_into(rh.at[2], part(3, 0))
        g_v(4, rh.at[2]).start()
        g_h(0, rh.at[0]).wait_recv()
        add_into(rh.at[0], part(1, 0))
        g_v(2, rh.at[0]).start()

    for d in (1, 2, 3):
        there = frag.at[lax.rem(zh + 4 - d, 4), x]
        remote(there, there, za_s, za_r, d - 1, dev_zh[d - 1]).wait_recv()
    xa_sends = [remote(frag.at[:, x], frag.at[:, x], xa_s, xa_r, d - 1, dev_x[d - 1]) for d in (1, 2, 3)]
    for copy in xa_sends:
        copy.start()

    def wide(w, plane):
        return pl.ds(pl.multiple_of((ja, jb)[w] * 2 * ROWS + plane * ROWS, ROWS), ROWS)

    def key_term(w, plane, k):
        return jnp.dot(acts[:, wide(w, plane)], wbuf[(ja, jb)[w], plane, cols[k]], preferred_element_type=F32)

    def input_block(w, plane):
        j = (ja, jb)[w]
        for q in range(2):
            rows = pl.ds(q * HALF, HALF)
            total = nt_dot(cot[0], wbuf[j, plane, 0, rows]) + nt_dot(cot[1], wbuf[j, plane, 1, rows])
            at = j * 2 * ROWS + plane * ROWS + q * HALF
            ig_out[:, pl.ds(pl.multiple_of(at, HALF), HALF)] = total.astype(BF16)

    def from_sib(w, k):
        for q in range(2):
            w_from_sib(w, k, q).wait_recv()

    other = 1 - c
    key[1] = key_term(0, c, 1)
    from_sib(0, 1)
    key[1] += key_term(0, other, 1)

    @pl.when(near)
    def _():
        g_v(3, rv.at[3]).wait_recv()
        g_h(2, rh.at[2]).wait_recv()
        add_into(rv.at[3], rh.at[2])
        add_into(rv.at[3], part(2, 0))
        remote(rv.at[3], zr.at[0], z_s, z_r, 4, dev_z).start()
        w_v(0, *far_v[0]).wait_recv()
        w_sib(1, 0, 0).start()
        w_h(2, *near_h_in[2]).wait_recv()
        w_sib(1, 1, 1).start()

    @pl.when(far)
    def _():
        w_v(3, *near_v[3]).wait_recv()
        w_sib(0, 0, 1).start()
        w_h(2, *far_h_in[2]).wait_recv()
        w_sib(1, 1, 1).start()

    from_sib(0, 0)
    key[0] = key_term(0, c, 0)
    key[0] += key_term(0, other, 0)
    input_block(0, c)
    input_block(0, other)

    @pl.when(far)
    def _():
        w_h(1, *far_h_in[1]).wait_recv()
        w_sib(1, 1, 0).start()

    key[1] += key_term(1, c, 1)
    from_sib(1, 1)
    key_send[...] = (key[1] + key_term(1, other, 1)).astype(BF16)
    send_key = remote(key_send, key_recv, z_s, z_r, 3, dev_z)
    send_key.start()

    @pl.when(near)
    def _():
        g_v(4, rv.at[4]).wait_recv()
        add_into(rv.at[4], part(3, 0))
        remote(rv.at[4], zr.at[1], z_s, z_r, 5, dev_z).start()

    @pl.when(far)
    def _():
        w_v(4, *near_v[4]).wait_recv()
        w_sib(1, 0, 1).start()

    key[0] += key_term(1, c, 0)
    input_block(1, c)
    from_sib(1, 0)
    key[0] += key_term(1, other, 0)
    input_block(1, other)

    for d in (1, 2, 3):
        there = frag.at[:, lax.rem(x + 4 - d, 4)]
        remote(there, there, xa_s, xa_r, d - 1, dev_x[d - 1]).wait_recv()
    frag_out[...] = frag[...]

    @pl.when(near)
    def _():
        for q in range(2):
            g_v(1 + q, rv.at[1 + q]).wait_recv()
            g_h(q, rh.at[q]).wait_recv()
            total = rv[1 + q].astype(F32) + rh[q].astype(F32) + gsum[0, 0, q].astype(F32)
            wg_out[q] = total.astype(BF16)

    @pl.when(far)
    def _():
        for q in range(2):
            remote(zr.at[q], zr.at[q], z_s, z_r, 4 + q, dev_z).wait_recv()
            wg_out[q] = zr[q]

    send_key.wait_recv()
    key_out[...] = (key[0] + key_recv[...].astype(F32)).astype(BF16)

    for copy in (send_cot, send_key, *send_g.values(), *x_sends, *z_sends, *za_sends, *xa_sends):
        copy.wait_send()
    for w in range(2):
        for k in range(2):
            for q in range(2):
                w_sib(w, k, q).wait_send()
    for i in range(3):
        g_h(i, rh.at[i]).wait_send()

    @pl.when(near)
    def _():
        for i in range(5):
            w_v(i, *near_v[i]).wait_send()
        for i in range(3):
            w_h(i, *near_h[i]).wait_send()
        g_v(0, rv.at[0]).wait_send()
        for q in range(2):
            remote(rv.at[3 + q], zr.at[q], z_s, z_r, 4 + q, dev_z).wait_send()

    @pl.when(far)
    def _():
        w_v(0, *far_v[0]).wait_send()
        for i in range(3):
            w_h(i, *far_h[i]).wait_send()
        for i in range(5):
            g_v(i, rv.at[i]).wait_send()
        for q in range(2):
            w_to_z(q).wait_send()


def deliver(*refs):
    sem = refs[-1]
    half = len(refs) // 2
    copies = []
    for i in range(half):
        if i == 1:
            for n in range(4):
                rows = pl.ds(n * (TOK // 4), TOK // 4)
                copies.append((refs[i].at[rows], refs[half + i].at[rows]))
        else:
            copies.append((refs[i], refs[half + i]))
    copies = [pltpu.make_async_copy(a, b, sem.at[i]) for i, (a, b) in enumerate(copies)]
    for copy in copies:
        copy.start()
    for copy in copies:
        copy.wait()


def local(
    activations, key_weight, key_cotangent, outer_mantissa, outer_exponent, round_index, global_weight, outer_momentum
):
    vmem = pltpu.VMEM
    dma = lambda n: pltpu.SemaphoreType.DMA((n,))
    exponent = jnp.transpose(outer_exponent[0], (0, 2, 1))
    anywhere = pl.BlockSpec(memory_space=pl.ANY)
    hold = lambda v: pltpu.with_memory_space_constraint(v, pltpu.HBM)
    near_by = pl.BlockSpec(memory_space=pltpu.VMEM)
    outs = pl.pallas_call(
        kernel,
        out_shape=(
            jax.ShapeDtypeStruct((TOK, COLS), BF16),
            jax.ShapeDtypeStruct((TOK, WIDTH), BF16),
            jax.ShapeDtypeStruct((2, HALF, COLS), BF16),
            jax.ShapeDtypeStruct((FRAGS, STATE, COLS), F32),
            jax.ShapeDtypeStruct((FRAGS, STATE, COLS), F32),
            jax.ShapeDtypeStruct((4, 4, STATE, COLS), BF16),
        ),
        in_specs=[anywhere] * 5 + [pl.BlockSpec(memory_space=pltpu.SMEM)] + [anywhere] * 2,
        out_specs=[near_by] * 6,
        scratch_shapes=[
            vmem((TOK, WIDTH), BF16),
            vmem((2, TOK, COLS), BF16),
            vmem((2, 2, 2, ROWS, COLS), BF16),
            vmem((2, 2, 2, HALF, COLS), BF16),
            vmem((2, 2, 2, HALF, COLS), BF16),
            vmem((2, 2, 2, HALF, COLS), BF16),
            vmem((5, HALF, COLS), BF16),
            vmem((3, HALF, COLS), BF16),
            vmem((2, HALF, COLS), BF16),
            vmem((2, TOK, COLS), F32),
            vmem((TOK, COLS), BF16),
            vmem((TOK, COLS), BF16),
            vmem((FRAGS, ROWS, COLS), BF16),
            vmem((FRAGS, 2, ROWS), jnp.int32),
            vmem((4, 4, STATE, COLS), BF16),
            vmem((3, 4, STATE, COLS), BF16),
            vmem((4, STATE, COLS), BF16),
            vmem((3, STATE, COLS), BF16),
            vmem((4, 4, STATE, COLS), BF16),
            vmem((FRAGS, STATE, COLS), F32),
            vmem((FRAGS, STATE, COLS), F32),
            dma(len(LOADS)),
            dma(5), dma(5), dma(3), dma(3), dma(5), dma(5), dma(3), dma(3),
            dma(8), dma(8), dma(4), dma(4), dma(6), dma(6),
            dma(3), dma(3), dma(3), dma(3), dma(3), dma(3), dma(3), dma(3),
        ],
        compiler_params=pltpu.CompilerParams(
            collective_id=0, has_side_effects=True, vmem_limit_bytes=44 * 2**20
        ),
    )(
        hold(activations), hold(key_weight[0]), hold(key_cotangent), hold(outer_mantissa[0]), hold(exponent),
        round_index, hold(global_weight), hold(outer_momentum),
    )
    outs = pl.pallas_call(
        deliver,
        out_shape=tuple(jax.ShapeDtypeStruct(o.shape, o.dtype) for o in outs),
        in_specs=[anywhere] * 6,
        out_specs=[anywhere] * 6,
        scratch_shapes=[dma(9)],
        compiler_params=pltpu.CompilerParams(vmem_limit_bytes=2**20),
    )(*outs)
    key_states, input_grad, weight_grad, global_weight_out, momentum_out, fragment_weight = outs
    return (
        key_states,
        input_grad,
        weight_grad.reshape(1, ROWS, COLS),
        global_weight_out,
        momentum_out,
        fragment_weight.reshape(ROWS, COLS),
    )


def solution(mesh):
    placed = (
        P(("replica", "fsdp"), "tensor"),
        P("replica", "fsdp", "tensor"),
        P(("replica", "fsdp"), "tensor"),
        P("replica", None, "fsdp", "tensor"),
        P("replica", None, "fsdp", "tensor"),
        P(),
        P(None, ("fsdp", "replica"), "tensor"),
        P(None, ("fsdp", "replica"), "tensor"),
    )
    return jax.shard_map(
        local,
        mesh=mesh,
        in_specs=placed,
        out_specs=(
            P(("replica", "fsdp"), "tensor"),
            P(("replica", "fsdp"), "tensor"),
            P("replica", "fsdp", "tensor"),
            P(None, ("fsdp", "replica"), "tensor"),
            P(None, ("fsdp", "replica"), "tensor"),
            P("fsdp", "tensor"),
        ),
        check_vma=False,
    )
```

time: 74.1 us -> 62.1 us (0.84)
  the two profiles are of different devices: /device:TPU:32 before, /device:TPU:14 now
where the time goes in v2:
time: 62.1 us; the launch traced here: 62 us
  Pallas kernels  60.7 us (98%)
  between operations  1.29 us (2%)
    pallas_call x1, Pallas kernels, local(): pl.pallas_call(kernel, out_shape=(jax.ShapeDtypeStruct((TOK, COLS), BF16)...  58.4 us
    pallas_call x1, Pallas kernels, local(): pl.pallas_call(deliver, out_shape=tuple((jax.ShapeDtypeStruct(o.shape, o....  2.32 us

profile of v2, /device:TPU:14, one launch (start us, length us, event | category | flops | bytes accessed | tf_op | source)
XLA Modules:
  0.0 62.0 jit_solution(16450300153036636129)
XLA Ops:
  1.3 58.4 %shard_map.127 = (bf16[384,256]{1,0:T(8,128)(2,1)S(1)}, bf16[384,4096]{1,0:T(8,128)(2,1)S(1)}, bf16[2,512,256]{2,1,0:T(8,128)(2,1)S(1)}, f32[4,64,256]{2,1,0:T(8...) custom-call(bf16[384,4096]{1,0:T(8,128)(2,1)} %acts_hbm.1, bf16[1024,256]{1,0:T(8,128)(2,1)} %bitcast.8, ...), custom_call_target="tpu_custom_call" | custom-call | tf_op jit(solution)/shard_map/pallas_call | solution.py:476
  59.7 2.3 %shard_map.128 = (bf16[384,256]{1,0:T(8,128)(2,1)}, bf16[384,4096]{1,0:T(8,128)(2,1)}, bf16[2,512,256]{2,1,0:T(8,128)(2,1)}, f32[4,64,256]{2,1,0:T(8,128)}, f32[...) custom-call(bf16[384,256]{1,0:T(8,128)(2,1)S(1)} %get-tuple-element.18.refs_0_, ...), custom_call_target="tpu_custom_call" | custom-call | tf_op jit(solution)/shard_map/pallas_call | solution.py:522

commit v3 on v0

v3 whole, which is shorter than its diff:
```python
import jax
import jax.numpy as jnp
from jax import lax
from jax.experimental import pallas as pl
from jax.experimental.pallas import tpu as pltpu
from jax.sharding import PartitionSpec as P

MESH = pl.DeviceIdType.MESH
F32 = jnp.float32
BF16 = jnp.bfloat16

TOK = 384
ROWS = 1024
COLS = 256
WIDTH = 4096
STATE = 64
FRAGS = 4
RATE = 0.7
BETA = 0.9
PIECES = 4
PIECE = ROWS // PIECES
WEIGHT_ROUTE = ((2, 1, 2, 4), (2, 4, 1, 2))
GRAD_ROUTE = ((2, 1, 4, 1), (2, 4, 2, 2))
LOADS = ("cot", "weight", "acts", "mant", "expo", "gw", "mom")

STEPS = (
    "Gs00", "Gs01", "Gs02", "Gs03", "Gk00", "Gk01", "Gk02", "Gk03", "O1",
    "Gs10", "Gs11", "Gs12", "Gs13", "Gk10", "Gk11", "Gk12", "Gk13", "O2", "O3", "Ka0",
    "Ka1", "O4", "Kb", "Kc", "Kd0", "Kd1", "Ke0", "Ke1", "O5", "Kf",
)
NEAR = (
    (
        ("cot", 0, 0, 0), ("s", 0, 0, 1), ("s", 0, 0, 0), ("v", 0, 0, 2), ("s", 0, 0, 2), ("h", 0, 0, 0),
    ),
    (),
    (),
    (),
    (
        ("s", 0, 0, 3), ("v", 0, 0, 3), ("h", 0, 0, 2),
    ),
    (),
    (),
    (),
    (),
    (
        ("gv", 1, 0, 2), ("s", 1, 0, 0),
    ),
    (),
    (),
    (),
    (
        ("gh", 1, 0, 0),
    ),
    (
        ("s", 1, 0, 2),
    ),
    (
        ("gv", 1, 1, 1), ("s", 0, 1, 0),
    ),
    (
        ("gh", 1, 1, 0),
    ),
    (
        ("v", 0, 1, 0), ("s", 0, 1, 1), ("h", 0, 1, 0),
    ),
    (
        ("v", 0, 1, 1), ("s", 0, 1, 2), ("h", 0, 1, 2), ("f", 0, 0, 0), ("s", 1, 1, 0), ("v", 0, 1, 2),
        ("s", 0, 1, 3), ("h", 0, 1, 3), ("f", 0, 1, 0), ("s", 1, 1, 2), ("v", 1, 1, 2), ("gh", 1, 1, 2),
    ),
    (),
    (),
    (
        ("s", 1, 1, 3), ("v", 0, 1, 3), ("gh", 1, 0, 1), ("f", 0, 1, 1), ("v", 0, 0, 1), ("h", 0, 0, 1),
        ("f", 0, 1, 2),
    ),
    (
        ("f", 0, 0, 1), ("v", 0, 0, 0), ("gh", 1, 1, 3), ("s", 1, 1, 1), ("s", 1, 0, 1),
    ),
    (
        ("v", 1, 0, 1),
    ),
    (),
    (),
    (
        ("gh", 1, 0, 3), ("f", 0, 1, 3),
    ),
    (
        ("s", 1, 0, 3), ("f", 0, 0, 3),
    ),
    (),
    (),
    (
        ("f", 0, 0, 2),
    ),
)
FAR = (
    (
        ("cot", 0, 0, 0),
    ),
    (),
    (),
    (),
    (),
    (
        ("gh", 1, 0, 0),
    ),
    (
        ("gv", 1, 0, 1), ("z", 0, 1, 0),
    ),
    (),
    (),
    (
        ("h", 0, 0, 2), ("s", 0, 0, 2),
    ),
    (),
    (),
    (),
    (
        ("gv", 0, 0, 3), ("z", 0, 1, 1),
    ),
    (
        ("s", 0, 0, 3),
    ),
    (
        ("gh", 1, 1, 0),
    ),
    (
        ("gv", 0, 0, 1),
    ),
    (
        ("z", 0, 1, 2), ("s", 1, 0, 2), ("gh", 1, 1, 2), ("gv", 0, 0, 0), ("z", 0, 1, 3),
    ),
    (
        ("gh", 1, 1, 1), ("gv", 0, 1, 0), ("s", 0, 1, 0), ("gh", 1, 1, 3), ("gv", 0, 1, 2), ("s", 0, 1, 1),
        ("h", 0, 1, 1), ("gv", 0, 1, 1),
    ),
    (
        ("s", 0, 1, 2), ("h", 0, 1, 0), ("gv", 0, 1, 3), ("f", 0, 1, 0), ("s", 1, 1, 1), ("s", 1, 1, 2),
        ("h", 0, 0, 3), ("v", 1, 1, 1), ("s", 1, 1, 0), ("s", 0, 1, 3),
    ),
    (
        ("h", 0, 1, 3), ("gv", 1, 0, 3),
    ),
    (),
    (
        ("f", 0, 1, 1), ("s", 1, 0, 3), ("s", 0, 0, 1), ("gh", 1, 0, 2), ("v", 1, 0, 3), ("f", 0, 1, 2),
        ("s", 1, 1, 3),
    ),
    (
        ("s", 0, 0, 0), ("h", 0, 0, 0),
    ),
    (),
    (),
    (
        ("gv", 0, 0, 2), ("s", 1, 0, 1), ("s", 1, 0, 0),
    ),
    (),
    (),
    (),
    (
        ("f", 0, 1, 3),
    ),
)


def tt_dot(a, b):
    return lax.dot_general(a, b, (((0,), (0,)), ((), ())), preferred_element_type=F32)


def nt_dot(a, b):
    return lax.dot_general(a, b, (((1,), (1,)), ((), ())), preferred_element_type=F32)


def kernel(
    acts_hbm, weight_hbm, cot_hbm, mant_hbm, expo_hbm, round_ref, gw_hbm, mom_hbm,
    key_out, ig_out, wg_out, gw_out, mom_out, frag_out,
    acts, cot, wbuf, gsend, grecv, gsum, rv, rh, zr, key, key_send, key_recv,
    mant, expo, contrib, xr, xsum, zrecv, frag, gw, mom,
    ld, wv_s, wv_r, wh_s, wh_r, rv_s, rv_r, rh_s, rh_r, bw_s, bw_r, bg_s, bg_r, z_s, z_r,
    xs_s, xs_r, zs_s, zs_r, za_s, za_r, xa_s, xa_r,
):
    r = lax.axis_index("replica")
    f = lax.axis_index("fsdp")
    t = lax.axis_index("tensor")
    zh, x = r // 4, lax.rem(r, 4)
    y, c = f // 2, lax.rem(f, 2)
    odd = lax.rem(y, 2)
    near = (y // 2) == t
    far = (y // 2) != t
    ja = jnp.where(near, odd, 1 - odd)
    column = (ja, 1 - ja)
    cols = (t, 1 - t)
    dev_h = (r, (y + 1 - 2 * odd) * 2 + c, t)
    dev_v = (r, (3 - y) * 2 + c, t)
    dev_z = (r, f, 1 - t)
    dev_s = (r, y * 2 + 1 - c, t)
    dev_x = [(zh * 4 + lax.rem(x + d, 4), f, t) for d in (1, 2, 3)]
    dev_zh = [(lax.rem(zh + d, 4) * 4 + x, f, t) for d in (1, 2, 3)]

    barrier = pltpu.get_barrier_semaphore()
    everyone = [dev_h, dev_v, dev_z, dev_s, *dev_x, *dev_zh]
    for device in everyone:
        pl.semaphore_signal(barrier, inc=1, device_id=device, device_id_type=MESH)

    def load(name, src, dst):
        return pltpu.make_async_copy(src, dst, ld.at[LOADS.index(name)])

    def remote(src, dst, s, r_, i, device):
        return pltpu.make_async_remote_copy(
            src_ref=src, dst_ref=dst, send_sem=s.at[i], recv_sem=r_.at[i], device_id=device, device_id_type=MESH
        )

    load_cot = load("cot", cot_hbm, cot.at[t])
    load_weight = load("weight", weight_hbm, wbuf.at[ja, c, t])
    load_acts = load("acts", acts_hbm, acts)
    load_mant = load("mant", mant_hbm, mant)
    load_expo = load("expo", expo_hbm, expo)
    load_gw = load("gw", gw_hbm, gw)
    load_mom = load("mom", mom_hbm, mom)
    load_cot.start()

    @pl.when(near)
    def _():
        load_weight.start()

    for one in (load_acts, load_mant, load_expo, load_gw, load_mom):
        one.start()

    def piece(w, plane, k, q):
        return wbuf.at[column[w], plane, cols[k], pl.ds(q * PIECE, PIECE)]

    def at(w, k, q):
        return (w * 2 + k) * PIECES + q

    def part(w, k, q):
        return gsum.at[k, w, q]

    def from_sib(w, k, q):
        there = piece(w, 1 - c, k, q)
        return remote(there, there, bw_s, bw_r, at(w, k, q), dev_s)

    def copy_of(name, w, k, q):
        if name == "v":
            return remote(piece(w, c, k, q), piece(w, c, k, q), wv_s, wv_r, at(w, k, q), dev_v)
        if name == "h":
            return remote(piece(w, c, k, q), piece(w, c, k, q), wh_s, wh_r, at(0, k, q), dev_h)
        if name == "s":
            return remote(piece(w, c, k, q), piece(w, c, k, q), bw_s, bw_r, at(w, k, q), dev_s)
        if name == "z":
            rows = pl.ds(q * PIECE, PIECE)
            return remote(weight_hbm.at[rows], wbuf.at[odd, c, t, rows], z_s, z_r, 2 + q, dev_z)
        if name == "gv":
            src = part(w, k, q)
            if w == 0 and GRAD_ROUTE[k][q] != 1:
                src = rh.at[k, q]
            return remote(src, rv.at[w, k, q], rv_s, rv_r, at(w, k, q), dev_v)
        if name == "f":
            return remote(rv.at[0, k, q], zr.at[q], z_s, z_r, 2 + PIECES + q, dev_z)
        return remote(cot.at[t], cot.at[t], z_s, z_r, 0, dev_z)

    def grad_h(is_near, k, q):
        route = GRAD_ROUTE[k][q]
        src = rv.at[1, k, q] if route == (1 if is_near else 4) else part(1, k, q)
        return remote(src, rh.at[k, q], rh_s, rh_r, at(0, k, q), dev_h)

    def add_into(dst, *others):
        total = dst[...].astype(F32)
        for other in others:
            total = total + other[...].astype(F32)
        dst[...] = total.astype(BF16)

    class Role:
        def __init__(self, is_near):
            self.is_near = is_near
            self.seen = set()

        def once(self, key, *copy):
            if key not in self.seen:
                self.seen.add(key)
                remote(*copy).wait_recv()

        def have(self, w, k, q):
            there = piece(w, c, k, q)
            if self.is_near and w == 0:
                if k == 0:
                    if "weight" not in self.seen:
                        self.seen.add("weight")
                        load_weight.wait()
                else:
                    self.once(("z", q), there, there, z_s, z_r, 2 + q, dev_z)
                return
            over_v = (WEIGHT_ROUTE[k][q] == 4) if self.is_near else (w == 0 or WEIGHT_ROUTE[k][q] == 1)
            if over_v:
                self.once(("v", w, k, q), there, there, wv_s, wv_r, at(w, k, q), dev_v)
            else:
                self.once(("h", w, k, q), there, there, wh_s, wh_r, at(0, k, q), dev_h)

        def have_v(self, w, k, q):
            there = rv.at[w, k, q]
            self.once(("gv", w, k, q), there, there, rv_s, rv_r, at(w, k, q), dev_v)

        def have_h(self, k, q):
            there = rh.at[k, q]
            self.once(("gh", k, q), there, there, rh_s, rh_r, at(0, k, q), dev_h)

        def copy(self, name, w, k, q):
            return grad_h(self.is_near, k, q) if name == "gh" else copy_of(name, w, k, q)

        def do(self, name, w, k, q):
            if name in ("v", "h", "s"):
                self.have(w, k, q)
            elif name == "cot":
                load_cot.wait()
            elif name == "gh":
                if GRAD_ROUTE[k][q] == (1 if self.is_near else 4):
                    self.have_v(1, k, q)
                    add_into(rv.at[1, k, q], part(1, k, q))
            elif name == "gv":
                if w == 0 and GRAD_ROUTE[k][q] != 1:
                    self.have_h(k, q)
                    add_into(rh.at[k, q], part(0, k, q))
            elif name == "f":
                if not self.is_near:
                    remote(zr.at[q], zr.at[q], z_s, z_r, 2 + PIECES + q, dev_z).wait_recv()
                    wg_out[q] = zr[q]
                    return
                self.have_v(0, k, q)
                terms = [part(0, k, q)]
                if GRAD_ROUTE[k][q] != 4:
                    self.have_h(k, q)
                    terms.append(rh.at[k, q])
                add_into(rv.at[0, k, q], *terms)
                if k == 0:
                    wg_out[q] = rv[0, k, q]
                    return
            self.copy(name, w, k, q).start()

        def sent(self, name, w, k, q):
            return not (name == "f" and (k == 0 or not self.is_near))

    roles = ((near, Role(True), NEAR), (far, Role(False), FAR))
    chosen = lax.rem(round_ref[0], FRAGS)
    other = 1 - c

    def grad_block(k, w, plane, q):
        first = column[w] * 2 * ROWS + plane * ROWS + q * PIECE
        return tt_dot(acts[:, pl.ds(pl.multiple_of(first, PIECE), PIECE)], cot[cols[k]])

    def grad_to_sib(k, q):
        return remote(gsend.at[k, q], grecv.at[k, q], bg_s, bg_r, k * PIECES + q, dev_s)

    def grad_send(k, q):
        if (k, q) == (0, 0):
            load_acts.wait()
        if (k, q) == (1, 0):
            remote(cot.at[1 - t], cot.at[1 - t], z_s, z_r, 0, dev_z).wait_recv()
        for w in range(2):
            gsend[k, q, w] = grad_block(k, w, other, q).astype(BF16)
        grad_to_sib(k, q).start()

    def grad_keep(k, q):
        grad_to_sib(k, q).wait_recv()
        for w in range(2):
            gsum[k, w, q] = (grad_block(k, w, c, q) + grecv[k, q, w].astype(F32)).astype(BF16)

    def x_send(d):
        return remote(contrib.at[:, lax.rem(x + d, 4)], xr.at[d - 1], xs_s, xs_r, d - 1, dev_x[d - 1])

    def z_send(d):
        return remote(xsum.at[lax.rem(zh + d, 4)], zrecv.at[d - 1], zs_s, zs_r, d - 1, dev_zh[d - 1])

    def z_back(d):
        return remote(frag.at[zh, x], frag.at[zh, x], za_s, za_r, d - 1, dev_zh[d - 1])

    def x_back(d):
        return remote(frag.at[:, x], frag.at[:, x], xa_s, xa_r, d - 1, dev_x[d - 1])

    def outer_1():
        load_mant.wait()
        load_expo.wait()
        power = jnp.exp2(expo[chosen].astype(F32))
        power = jnp.transpose(jnp.concatenate([power] * 4, axis=0))
        for h in range(2):
            block = mant[chosen, :, h * 128 : (h + 1) * 128].astype(F32) * power[:, h : h + 1]
            contrib[:, :, :, h * 128 : (h + 1) * 128] = block.astype(BF16).reshape(4, 4, STATE, 128)
        for d in (1, 2, 3):
            x_send(d).start()

    def outer_2():
        for d in (1, 2, 3):
            x_send(d).wait_recv()
        for i in range(4):
            total = contrib[i, x].astype(F32)
            for d in range(3):
                total = total + xr[d, i].astype(F32)
            xsum[i] = total.astype(BF16)
        for d in (1, 2, 3):
            z_send(d).start()

    def outer_3():
        load_gw.wait()
        load_mom.wait()
        for d in (1, 2, 3):
            z_send(d).wait_recv()
        total = xsum[zh].astype(F32)
        for d in range(3):
            total = total + zrecv[d].astype(F32)
        delta = total * (1.0 / 16)
        new_moment = BETA * mom[chosen] + delta
        new_weight = gw[chosen] - RATE * (delta + BETA * new_moment)
        for i in range(FRAGS):
            mom_out[i] = jnp.where(chosen == i, new_moment, mom[i])
            gw_out[i] = jnp.where(chosen == i, new_weight, gw[i])
        frag[zh, x] = new_weight.astype(BF16)
        for d in (1, 2, 3):
            z_back(d).start()

    def outer_4():
        for d in (1, 2, 3):
            there = frag.at[lax.rem(zh + 4 - d, 4), x]
            remote(there, there, za_s, za_r, d - 1, dev_zh[d - 1]).wait_recv()
        for d in (1, 2, 3):
            x_back(d).start()

    def outer_5():
        for d in (1, 2, 3):
            there = frag.at[:, lax.rem(x + 4 - d, 4)]
            remote(there, there, xa_s, xa_r, d - 1, dev_x[d - 1]).wait_recv()
        frag_out[...] = frag[...]

    def key_term(w, plane, k):
        wide = pl.ds(pl.multiple_of(column[w] * 2 * ROWS + plane * ROWS, ROWS), ROWS)
        return jnp.dot(acts[:, wide], wbuf[column[w], plane, cols[k]], preferred_element_type=F32)

    def input_block(w, plane):
        for i in range(2):
            rows = pl.ds(i * 512, 512)
            total = nt_dot(cot[0], wbuf[column[w], plane, 0, rows]) + nt_dot(cot[1], wbuf[column[w], plane, 1, rows])
            first = column[w] * 2 * ROWS + plane * ROWS + i * 512
            ig_out[:, pl.ds(pl.multiple_of(first, 512), 512)] = total.astype(BF16)

    def sib_pieces(w, k):
        for q in range(PIECES):
            from_sib(w, k, q).wait_recv()

    send_key = remote(key_send, key_recv, z_s, z_r, 1, dev_z)

    def step(name):
        if name[0] == "G":
            (grad_send if name[1] == "s" else grad_keep)(int(name[2]), int(name[3]))
        elif name[0] == "O":
            (outer_1, outer_2, outer_3, outer_4, outer_5)[int(name[1]) - 1]()
        elif name == "Ka0":
            key[1] = key_term(0, c, 1)
        elif name == "Ka1":
            sib_pieces(0, 1)
            key[1] += key_term(0, other, 1)
        elif name == "Kb":
            key[1] += key_term(1, c, 1)
        elif name == "Kc":
            sib_pieces(1, 1)
            key_send[...] = (key[1] + key_term(1, other, 1)).astype(BF16)
            send_key.start()
        elif name == "Kd0":
            key[0] = key_term(0, c, 0)
            input_block(0, c)
        elif name == "Kd1":
            sib_pieces(0, 0)
            key[0] += key_term(0, other, 0)
            input_block(0, other)
        elif name == "Ke0":
            key[0] += key_term(1, c, 0)
            input_block(1, c)
        elif name == "Ke1":
            sib_pieces(1, 0)
            key[0] += key_term(1, other, 0)
            input_block(1, other)
        else:
            send_key.wait_recv()
            key_out[...] = (key[0] + key_recv[...].astype(F32)).astype(BF16)

    own_pieces = {"Ka0": (0, 1), "Kb": (1, 1), "Kd0": (0, 0), "Ke0": (1, 0)}

    pl.semaphore_wait(barrier, len(everyone))
    for i, name in enumerate((*STEPS, None)):
        for here, role, plan in roles:

            @pl.when(here)
            def _(role=role, tasks=plan[i], name=name):
                for task in tasks:
                    role.do(*task)
                if name in own_pieces:
                    for q in range(PIECES):
                        role.have(*own_pieces[name], q)

        if name is not None:
            step(name)

    send_key.wait_send()
    for d in (1, 2, 3):
        for copy in (x_send(d), z_send(d), z_back(d), x_back(d)):
            copy.wait_send()
    for k in range(2):
        for q in range(PIECES):
            grad_to_sib(k, q).wait_send()
    for here, role, plan in roles:

        @pl.when(here)
        def _(role=role, plan=plan):
            for tasks in plan:
                for task in tasks:
                    if role.sent(*task):
                        role.copy(*task).wait_send()


def deliver(*refs):
    sem = refs[-1]
    half = len(refs) // 2
    pairs = list(zip(refs[:half], refs[half:-1]))
    ig, ig_out = pairs.pop(1)
    quarter = TOK // 4
    for n in range(4):
        rows = pl.ds(n * quarter, quarter)
        pairs.append((ig.at[rows], ig_out.at[rows]))
    copies = [pltpu.make_async_copy(a, b, sem.at[i]) for i, (a, b) in enumerate(pairs)]
    for copy in copies:
        copy.start()
    for copy in copies:
        copy.wait()


def local(
    activations, key_weight, key_cotangent, outer_mantissa, outer_exponent, round_index, global_weight, outer_momentum
):
    vmem = pltpu.VMEM
    dma = lambda n: pltpu.SemaphoreType.DMA((n,))
    hold = lambda v: pltpu.with_memory_space_constraint(v, pltpu.HBM)
    exponent = jnp.transpose(outer_exponent[0], (0, 2, 1))
    anywhere = pl.BlockSpec(memory_space=pl.ANY)
    near_by = pl.BlockSpec(memory_space=pltpu.VMEM)
    n = PIECES
    outs = pl.pallas_call(
        kernel,
        out_shape=(
            jax.ShapeDtypeStruct((TOK, COLS), BF16),
            jax.ShapeDtypeStruct((TOK, WIDTH), BF16),
            jax.ShapeDtypeStruct((n, PIECE, COLS), BF16),
            jax.ShapeDtypeStruct((FRAGS, STATE, COLS), F32),
            jax.ShapeDtypeStruct((FRAGS, STATE, COLS), F32),
            jax.ShapeDtypeStruct((4, 4, STATE, COLS), BF16),
        ),
        in_specs=[anywhere] * 5 + [pl.BlockSpec(memory_space=pltpu.SMEM)] + [anywhere] * 2,
        out_specs=[near_by] * 6,
        scratch_shapes=[
            vmem((TOK, WIDTH), BF16),
            vmem((2, TOK, COLS), BF16),
            vmem((2, 2, 2, ROWS, COLS), BF16),
            vmem((2, n, 2, PIECE, COLS), BF16),
            vmem((2, n, 2, PIECE, COLS), BF16),
            vmem((2, 2, n, PIECE, COLS), BF16),
            vmem((2, 2, n, PIECE, COLS), BF16),
            vmem((2, n, PIECE, COLS), BF16),
            vmem((n, PIECE, COLS), BF16),
            vmem((2, TOK, COLS), F32),
            vmem((TOK, COLS), BF16),
            vmem((TOK, COLS), BF16),
            vmem((FRAGS, ROWS, COLS), BF16),
            vmem((FRAGS, 2, ROWS), jnp.int32),
            vmem((4, 4, STATE, COLS), BF16),
            vmem((3, 4, STATE, COLS), BF16),
            vmem((4, STATE, COLS), BF16),
            vmem((3, STATE, COLS), BF16),
            vmem((4, 4, STATE, COLS), BF16),
            vmem((FRAGS, STATE, COLS), F32),
            vmem((FRAGS, STATE, COLS), F32),
            dma(len(LOADS)),
            dma(4 * n), dma(4 * n), dma(2 * n), dma(2 * n), dma(4 * n), dma(4 * n), dma(2 * n), dma(2 * n),
            dma(4 * n), dma(4 * n), dma(2 * n), dma(2 * n), dma(2 + 2 * n), dma(2 + 2 * n),
            dma(3), dma(3), dma(3), dma(3), dma(3), dma(3), dma(3), dma(3),
        ],
        compiler_params=pltpu.CompilerParams(
            collective_id=0, has_side_effects=True, vmem_limit_bytes=44 * 2**20
        ),
    )(
        hold(activations), hold(key_weight[0]), hold(key_cotangent), hold(outer_mantissa[0]), hold(exponent),
        round_index, hold(global_weight), hold(outer_momentum),
    )
    outs = pl.pallas_call(
        deliver,
        out_shape=tuple(jax.ShapeDtypeStruct(o.shape, o.dtype) for o in outs),
        in_specs=[anywhere] * 6,
        out_specs=[anywhere] * 6,
        scratch_shapes=[dma(9)],
        compiler_params=pltpu.CompilerParams(vmem_limit_bytes=2**20),
    )(*outs)
    key_states, input_grad, weight_grad, global_weight_out, momentum_out, fragment_weight = outs
    return (
        key_states,
        input_grad,
        weight_grad.reshape(1, ROWS, COLS),
        global_weight_out,
        momentum_out,
        fragment_weight.reshape(ROWS, COLS),
    )


def solution(mesh):
    placed = (
        P(("replica", "fsdp"), "tensor"),
        P("replica", "fsdp", "tensor"),
        P(("replica", "fsdp"), "tensor"),
        P("replica", None, "fsdp", "tensor"),
        P("replica", None, "fsdp", "tensor"),
        P(),
        P(None, ("fsdp", "replica"), "tensor"),
        P(None, ("fsdp", "replica"), "tensor"),
    )
    return jax.shard_map(
        local,
        mesh=mesh,
        in_specs=placed,
        out_specs=(
            P(("replica", "fsdp"), "tensor"),
            P(("replica", "fsdp"), "tensor"),
            P("replica", "fsdp", "tensor"),
            P(None, ("fsdp", "replica"), "tensor"),
            P(None, ("fsdp", "replica"), "tensor"),
            P("fsdp", "tensor"),
        ),
        check_vma=False,
    )
```

time: 369 us -> 58.7 us (0.16)
  the two profiles are of different devices: /device:TPU:32 before, /device:TPU:1 now
where the time goes in v3:
time: 58.7 us
  Pallas kernels  57.4 us (98%)
  between operations  1.29 us (2%)
    pallas_call x1, Pallas kernels, local(): pl.pallas_call(kernel, out_shape=(jax.ShapeDtypeStruct((TOK, COLS), BF16)...  55 us
    pallas_call x1, Pallas kernels, local(): pl.pallas_call(deliver, out_shape=tuple((jax.ShapeDtypeStruct(o.shape, o....  2.32 us

profile of v3, /device:TPU:1, one launch (start us, length us, event | category | flops | bytes accessed | tf_op | source)
XLA Modules:
  0.0 58.7 jit_solution(14043670030309096879)
XLA Ops:
  1.3 55.0 %shard_map.127 = (bf16[384,256]{1,0:T(8,128)(2,1)S(1)}, bf16[384,4096]{1,0:T(8,128)(2,1)S(1)}, bf16[4,256,256]{2,1,0:T(8,128)(2,1)S(1)}, f32[4,64,256]{2,1,0:T(8...) custom-call(bf16[384,4096]{1,0:T(8,128)(2,1)} %acts_hbm.1, bf16[1024,256]{1,0:T(8,128)(2,1)} %bitcast.8, ...), custom_call_target="tpu_custom_call" | custom-call | tf_op jit(solution)/shard_map/pallas_call | solution.py:542
  56.3 2.3 %shard_map.128 = (bf16[384,256]{1,0:T(8,128)(2,1)}, bf16[384,4096]{1,0:T(8,128)(2,1)}, bf16[4,256,256]{2,1,0:T(8,128)(2,1)}, f32[4,64,256]{2,1,0:T(8,128)}, f32[...) custom-call(bf16[384,256]{1,0:T(8,128)(2,1)S(1)} %get-tuple-element.18.refs_0_, ...), custom_call_target="tpu_custom_call" | custom-call | tf_op jit(solution)/shard_map/pallas_call | solution.py:588

commit v4 on v3

--- a/solution.py
+++ b/solution.py
@@ -19,79 +19,82 @@
 BETA = 0.9
 PIECES = 4
 PIECE = ROWS // PIECES
-WEIGHT_ROUTE = ((2, 1, 2, 4), (2, 4, 1, 2))
-GRAD_ROUTE = ((2, 1, 4, 1), (2, 4, 2, 2))
+WEIGHT_ROUTE = ((1, 4, 4, 2), (1, 2, 2, 2))
+GRAD_ROUTE = ((2, 2, 4, 1), (2, 2, 1, 4))
 LOADS = ("cot", "weight", "acts", "mant", "expo", "gw", "mom")
 
 STEPS = (
-    "Gs00", "Gs01", "Gs02", "Gs03", "Gk00", "Gk01", "Gk02", "Gk03", "O1",
-    "Gs10", "Gs11", "Gs12", "Gs13", "Gk10", "Gk11", "Gk12", "Gk13", "O2", "O3", "Ka0",
-    "Ka1", "O4", "Kb", "Kc", "Kd0", "Kd1", "Ke0", "Ke1", "O5", "Kf",
+    "Gs00", "Gs01", "Gs02", "Gs03", "O1", "Gk00", "Gk01", "Gk02", "Gk03",
+    "Gs10", "Gs11", "Gs12", "Gs13", "Gk10", "Gk11", "Gk12", "Gk13", "O2", "Ka0", "Ka1",
+    "O3", "Kb", "Kc", "O4", "Kd0", "Kd1", "Ke0", "Ke1", "O5", "Kf",
 )
 NEAR = (
     (
-        ("cot", 0, 0, 0), ("s", 0, 0, 1), ("s", 0, 0, 0), ("v", 0, 0, 2), ("s", 0, 0, 2), ("h", 0, 0, 0),
-    ),
-    (),
-    (),
-    (),
-    (
-        ("s", 0, 0, 3), ("v", 0, 0, 3), ("h", 0, 0, 2),
-    ),
-    (),
-    (),
-    (),
-    (),
-    (
-        ("gv", 1, 0, 2), ("s", 1, 0, 0),
-    ),
-    (),
-    (),
-    (),
+        ("cot", 0, 0, 0), ("s", 0, 0, 3), ("s", 0, 0, 2), ("h", 0, 0, 0), ("s", 0, 0, 1), ("s", 0, 0, 0),
+    ),
+    (),
+    (),
+    (),
+    (),
+    (
+        ("v", 0, 0, 1), ("h", 0, 0, 3),
+    ),
+    (
+        ("v", 0, 0, 2),
+    ),
     (
         ("gh", 1, 0, 0),
     ),
-    (
-        ("s", 1, 0, 2),
-    ),
-    (
-        ("gv", 1, 1, 1), ("s", 0, 1, 0),
-    ),
-    (
-        ("gh", 1, 1, 0),
-    ),
-    (
-        ("v", 0, 1, 0), ("s", 0, 1, 1), ("h", 0, 1, 0),
-    ),
-    (
-        ("v", 0, 1, 1), ("s", 0, 1, 2), ("h", 0, 1, 2), ("f", 0, 0, 0), ("s", 1, 1, 0), ("v", 0, 1, 2),
-        ("s", 0, 1, 3), ("h", 0, 1, 3), ("f", 0, 1, 0), ("s", 1, 1, 2), ("v", 1, 1, 2), ("gh", 1, 1, 2),
-    ),
-    (),
-    (),
-    (
-        ("s", 1, 1, 3), ("v", 0, 1, 3), ("gh", 1, 0, 1), ("f", 0, 1, 1), ("v", 0, 0, 1), ("h", 0, 0, 1),
-        ("f", 0, 1, 2),
-    ),
-    (
-        ("f", 0, 0, 1), ("v", 0, 0, 0), ("gh", 1, 1, 3), ("s", 1, 1, 1), ("s", 1, 0, 1),
-    ),
-    (
-        ("v", 1, 0, 1),
-    ),
-    (),
-    (),
-    (
-        ("gh", 1, 0, 3), ("f", 0, 1, 3),
-    ),
-    (
-        ("s", 1, 0, 3), ("f", 0, 0, 3),
-    ),
-    (),
-    (),
-    (
-        ("f", 0, 0, 2),
-    ),
+    (),
+    (
+        ("s", 1, 0, 0),
+    ),
+    (),
+    (),
+    (),
+    (
+        ("gv", 1, 0, 2), ("gh", 1, 0, 1),
+    ),
+    (
+        ("s", 1, 0, 3),
+    ),
+    (
+        ("s", 0, 1, 0),
+    ),
+    (),
+    (
+        ("v", 0, 1, 0), ("gh", 1, 1, 0),
+    ),
+    (
+        ("s", 0, 1, 3), ("v", 0, 1, 3), ("h", 0, 1, 3), ("s", 0, 1, 1), ("f", 0, 0, 0), ("v", 0, 1, 1),
+        ("h", 0, 1, 0),
+    ),
+    (
+        ("f", 0, 0, 1), ("s", 0, 1, 2), ("v", 0, 1, 2), ("h", 0, 1, 2),
+    ),
+    (
+        ("s", 1, 1, 3), ("s", 1, 0, 1), ("gv", 1, 1, 3), ("h", 0, 1, 1), ("s", 1, 1, 0),
+    ),
+    (
+        ("f", 0, 1, 0), ("v", 1, 1, 0), ("gh", 1, 1, 1), ("s", 1, 1, 2), ("v", 0, 0, 3), ("gh", 1, 1, 2),
+    ),
+    (
+        ("s", 1, 1, 1), ("f", 0, 0, 2), ("v", 1, 0, 0),
+    ),
+    (
+        ("gh", 1, 0, 3), ("f", 0, 1, 1), ("v", 0, 0, 0),
+    ),
+    (),
+    (),
+    (),
+    (
+        ("f", 0, 0, 3), ("s", 1, 0, 2), ("f", 0, 1, 2),
+    ),
+    (
+        ("f", 0, 1, 3),
+    ),
+    (),
+    (),
 )
 FAR = (
     (
@@ -101,65 +104,67 @@
     (),
     (),
     (),
+    (),
     (
         ("gh", 1, 0, 0),
     ),
     (
-        ("gv", 1, 0, 1), ("z", 0, 1, 0),
-    ),
-    (),
-    (),
-    (
-        ("h", 0, 0, 2), ("s", 0, 0, 2),
-    ),
-    (),
-    (),
-    (),
-    (
-        ("gv", 0, 0, 3), ("z", 0, 1, 1),
-    ),
-    (
-        ("s", 0, 0, 3),
-    ),
-    (
-        ("gh", 1, 1, 0),
-    ),
-    (
-        ("gv", 0, 0, 1),
-    ),
-    (
-        ("z", 0, 1, 2), ("s", 1, 0, 2), ("gh", 1, 1, 2), ("gv", 0, 0, 0), ("z", 0, 1, 3),
-    ),
-    (
-        ("gh", 1, 1, 1), ("gv", 0, 1, 0), ("s", 0, 1, 0), ("gh", 1, 1, 3), ("gv", 0, 1, 2), ("s", 0, 1, 1),
-        ("h", 0, 1, 1), ("gv", 0, 1, 1),
-    ),
-    (
-        ("s", 0, 1, 2), ("h", 0, 1, 0), ("gv", 0, 1, 3), ("f", 0, 1, 0), ("s", 1, 1, 1), ("s", 1, 1, 2),
-        ("h", 0, 0, 3), ("v", 1, 1, 1), ("s", 1, 1, 0), ("s", 0, 1, 3),
-    ),
-    (
-        ("h", 0, 1, 3), ("gv", 1, 0, 3),
-    ),
-    (),
-    (
-        ("f", 0, 1, 1), ("s", 1, 0, 3), ("s", 0, 0, 1), ("gh", 1, 0, 2), ("v", 1, 0, 3), ("f", 0, 1, 2),
-        ("s", 1, 1, 3),
-    ),
-    (
-        ("s", 0, 0, 0), ("h", 0, 0, 0),
-    ),
-    (),
-    (),
-    (
-        ("gv", 0, 0, 2), ("s", 1, 0, 1), ("s", 1, 0, 0),
-    ),
-    (),
-    (),
-    (),
-    (
-        ("f", 0, 1, 3),
-    ),
+        ("gh", 1, 0, 1),
+    ),
+    (
+        ("z", 0, 1, 0),
+    ),
+    (
+        ("gv", 0, 0, 3), ("z", 0, 1, 3), ("gv", 1, 0, 3),
+    ),
+    (),
+    (),
+    (),
+    (
+        ("h", 0, 0, 1), ("s", 0, 0, 1),
+    ),
+    (
+        ("gv", 0, 0, 0),
+    ),
+    (
+        ("z", 0, 1, 1),
+    ),
+    (),
+    (
+        ("gh", 1, 1, 0), ("s", 0, 0, 2), ("z", 0, 1, 2), ("gv", 0, 0, 1),
+    ),
+    (
+        ("h", 0, 0, 2), ("s", 1, 0, 1), ("v", 1, 0, 1), ("gh", 1, 0, 2), ("s", 0, 1, 0), ("gv", 0, 1, 0),
+        ("gh", 1, 1, 1), ("s", 0, 1, 3), ("s", 1, 0, 2), ("gv", 1, 1, 2), ("h", 0, 1, 3), ("s", 0, 1, 1),
+        ("gv", 0, 0, 2), ("h", 0, 1, 1), ("s", 0, 1, 2),
+    ),
+    (
+        ("gv", 0, 1, 1),
+    ),
+    (),
+    (
+        ("h", 0, 1, 2), ("s", 1, 1, 3), ("v", 1, 0, 2), ("gh", 1, 1, 3), ("f", 0, 1, 0), ("s", 1, 1, 0),
+        ("s", 1, 1, 1), ("gv", 0, 1, 2), ("h", 0, 0, 3), ("s", 0, 0, 3),
+    ),
+    (
+        ("s", 1, 1, 2),
+    ),
+    (
+        ("s", 1, 0, 0), ("gv", 0, 1, 3),
+    ),
+    (
+        ("f", 0, 1, 1),
+    ),
+    (
+        ("s", 0, 0, 0), ("s", 1, 0, 3),
+    ),
+    (),
+    (),
+    (
+        ("f", 0, 1, 2), ("f", 0, 1, 3),
+    ),
+    (),
+    (),
 )
 
 
@@ -177,7 +182,7 @@
     acts, cot, wbuf, gsend, grecv, gsum, rv, rh, zr, key, key_send, key_recv,
     mant, expo, contrib, xr, xsum, zrecv, frag, gw, mom,
     ld, wv_s, wv_r, wh_s, wh_r, rv_s, rv_r, rh_s, rh_r, bw_s, bw_r, bg_s, bg_r, z_s, z_r,
-    xs_s, xs_r, zs_s, zs_r, za_s, za_r, xa_s, xa_r,
+    xs_s, xs_r, zs_s, zs_r, za_s, za_r, xa_s, xa_r, group_sem, go_sem, far_sem,
 ):
     r = lax.axis_index("replica")
     f = lax.axis_index("fsdp")
@@ -198,9 +203,18 @@
     dev_zh = [(lax.rem(zh + d, 4) * 4 + x, f, t) for d in (1, 2, 3)]
 
     barrier = pltpu.get_barrier_semaphore()
-    everyone = [dev_h, dev_v, dev_z, dev_s, *dev_x, *dev_zh]
-    for device in everyone:
-        pl.semaphore_signal(barrier, inc=1, device_id=device, device_id_type=MESH)
+
+    def tell(sem, *devices):
+        for device in devices:
+            pl.semaphore_signal(sem, inc=1, device_id=device, device_id_type=MESH)
+
+    @pl.when(c == 0)
+    def _():
+        tell(barrier, dev_h, dev_v, dev_z, *dev_x)
+
+    @pl.when(c == 1)
+    def _():
+        tell(barrier, dev_s)
 
     def load(name, src, dst):
         return pltpu.make_async_copy(src, dst, ld.at[LOADS.index(name)])
@@ -310,7 +324,7 @@
             if name in ("v", "h", "s"):
                 self.have(w, k, q)
             elif name == "cot":
-                load_cot.wait()
+                pass
             elif name == "gh":
                 if GRAD_ROUTE[k][q] == (1 if self.is_near else 4):
                     self.have_v(1, k, q)
@@ -349,13 +363,23 @@
     def grad_to_sib(k, q):
         return remote(gsend.at[k, q], grecv.at[k, q], bg_s, bg_r, k * PIECES + q, dev_s)
 
-    def grad_send(k, q):
-        if (k, q) == (0, 0):
-            load_acts.wait()
-        if (k, q) == (1, 0):
-            remote(cot.at[1 - t], cot.at[1 - t], z_s, z_r, 0, dev_z).wait_recv()
+    def grad_other(k, q):
         for w in range(2):
             gsend[k, q, w] = grad_block(k, w, other, q).astype(BF16)
+
+    def grad_send(k, q):
+        if k == 0:
+
+            @pl.when(c == 0)
+            def _():
+                if q == 0:
+                    load_acts.wait()
+                grad_other(k, q)
+
+        else:
+            if q == 0:
+                remote(cot.at[1 - t], cot.at[1 - t], z_s, z_r, 0, dev_z).wait_recv()
+            grad_other(k, q)
         grad_to_sib(k, q).start()
 
     def grad_keep(k, q):
@@ -375,7 +399,7 @@
     def x_back(d):
         return remote(frag.at[:, x], frag.at[:, x], xa_s, xa_r, d - 1, dev_x[d - 1])
 
-    def outer_1():
+    def outer_own():
         load_mant.wait()
         load_expo.wait()
         power = jnp.exp2(expo[chosen].astype(F32))
@@ -383,6 +407,11 @@
         for h in range(2):
             block = mant[chosen, :, h * 128 : (h + 1) * 128].astype(F32) * power[:, h : h + 1]
             contrib[:, :, :, h * 128 : (h + 1) * 128] = block.astype(BF16).reshape(4, 4, STATE, 128)
+    def outer_1():
+        @pl.when(c == 0)
+        def _():
+            outer_own()
+
         for d in (1, 2, 3):
             x_send(d).start()
 
@@ -394,6 +423,16 @@
             for d in range(3):
                 total = total + xr[d, i].astype(F32)
             xsum[i] = total.astype(BF16)
+
+        @pl.when(c == 1)
+        def _():
+            pl.semaphore_wait(barrier, len(dev_zh))
+            tell(far_sem, dev_s)
+
+        @pl.when(c == 0)
+        def _():
+            pl.semaphore_wait(far_sem, 1)
+
         for d in (1, 2, 3):
             z_send(d).start()
 
@@ -481,8 +520,30 @@
 
     own_pieces = {"Ka0": (0, 1), "Kb": (1, 1), "Kd0": (0, 0), "Ke0": (1, 0)}
 
-    pl.semaphore_wait(barrier, len(everyone))
+    load_cot.wait()
+
+    @pl.when(c == 0)
+    def _():
+        pl.semaphore_wait(barrier, 4 + len(dev_x))
+        tell(group_sem, dev_h, dev_v, dev_z, *dev_x)
+
+    @pl.when(c == 1)
+    def _():
+        load_acts.wait()
+        for q in range(PIECES):
+            grad_other(0, q)
+        outer_own()
+        pl.semaphore_wait(go_sem, 1)
+        tell(barrier, *dev_zh)
+
     for i, name in enumerate((*STEPS, None)):
+        if i == 1:
+
+            @pl.when(c == 0)
+            def _():
+                pl.semaphore_wait(group_sem, 3 + len(dev_x))
+                tell(go_sem, dev_s)
+
         for here, role, plan in roles:
 
             @pl.when(here)
@@ -577,6 +638,7 @@
             dma(4 * n), dma(4 * n), dma(2 * n), dma(2 * n), dma(4 * n), dma(4 * n), dma(2 * n), dma(2 * n),
             dma(4 * n), dma(4 * n), dma(2 * n), dma(2 * n), dma(2 + 2 * n), dma(2 + 2 * n),
             dma(3), dma(3), dma(3), dma(3), dma(3), dma(3), dma(3), dma(3),
+            pltpu.SemaphoreType.REGULAR, pltpu.SemaphoreType.REGULAR, pltpu.SemaphoreType.REGULAR,
         ],
         compiler_params=pltpu.CompilerParams(
             collective_id=0, has_side_effects=True, vmem_limit_bytes=44 * 2**20

time: 58.7 us -> 55.4 us (0.944)
  the two profiles are of different devices: /device:TPU:1 before, /device:TPU:32 now
where the time goes in v4:
time: 55.4 us; the launch traced here: 54.9 us
  Pallas kernels  53.6 us (97%)
  between operations  1.29 us (2%)
    pallas_call x1, Pallas kernels, local(): pl.pallas_call(kernel, out_shape=(jax.ShapeDtypeStruct((TOK, COLS), BF16)...  51.3 us
    pallas_call x1, Pallas kernels, local(): pl.pallas_call(deliver, out_shape=tuple((jax.ShapeDtypeStruct(o.shape, o....  2.32 us

profile of v4, /device:TPU:32, one launch (start us, length us, event | category | flops | bytes accessed | tf_op | source)
XLA Modules:
  0.0 54.9 jit_solution(2241864241385458047)
XLA Ops:
  1.3 51.3 %shard_map.127 = (bf16[384,256]{1,0:T(8,128)(2,1)S(1)}, bf16[384,4096]{1,0:T(8,128)(2,1)S(1)}, bf16[4,256,256]{2,1,0:T(8,128)(2,1)S(1)}, f32[4,64,256]{2,1,0:T(8...) custom-call(bf16[384,4096]{1,0:T(8,128)(2,1)} %acts_hbm.1, bf16[1024,256]{1,0:T(8,128)(2,1)} %bitcast.8, ...), custom_call_target="tpu_custom_call" | custom-call | tf_op jit(solution)/shard_map/pallas_call | solution.py:603
  52.6 2.3 %shard_map.128 = (bf16[384,256]{1,0:T(8,128)(2,1)}, bf16[384,4096]{1,0:T(8,128)(2,1)}, bf16[4,256,256]{2,1,0:T(8,128)(2,1)}, f32[4,64,256]{2,1,0:T(8,128)}, f32[...) custom-call(bf16[384,256]{1,0:T(8,128)(2,1)S(1)} %get-tuple-element.18.refs_0_, ...), custom_call_target="tpu_custom_call" | custom-call | tf_op jit(solution)/shard_map/pallas_call | solution.py:650

commit v5 on v4

--- a/solution.py
+++ b/solution.py
@@ -19,79 +19,70 @@
 BETA = 0.9
 PIECES = 4
 PIECE = ROWS // PIECES
-WEIGHT_ROUTE = ((1, 4, 4, 2), (1, 2, 2, 2))
-GRAD_ROUTE = ((2, 2, 4, 1), (2, 2, 1, 4))
+WEIGHT_ROUTE = ((4, 2, 2, 1), (2, 1, 2, 4))
+GRAD_ROUTE = ((2, 1, 4, 2), (2, 4, 1, 2))
 LOADS = ("cot", "weight", "acts", "mant", "expo", "gw", "mom")
 
 STEPS = (
     "Gs00", "Gs01", "Gs02", "Gs03", "O1", "Gk00", "Gk01", "Gk02", "Gk03",
-    "Gs10", "Gs11", "Gs12", "Gs13", "Gk10", "Gk11", "Gk12", "Gk13", "O2", "Ka0", "Ka1",
-    "O3", "Kb", "Kc", "O4", "Kd0", "Kd1", "Ke0", "Ke1", "O5", "Kf",
+    "Gs10", "Gs11", "Gs12", "Gs13", "Gk10", "Gk11", "Gk12", "Gk13", "O2", "O3", "Ka0",
+    "Ka1", "Kb", "Kc", "O4", "Kd0", "Kd1", "Ke0", "Ke1", "O5", "Kf",
 )
 NEAR = (
     (
-        ("cot", 0, 0, 0), ("s", 0, 0, 3), ("s", 0, 0, 2), ("h", 0, 0, 0), ("s", 0, 0, 1), ("s", 0, 0, 0),
-    ),
-    (),
-    (),
-    (),
-    (),
-    (
-        ("v", 0, 0, 1), ("h", 0, 0, 3),
-    ),
-    (
-        ("v", 0, 0, 2),
-    ),
-    (
-        ("gh", 1, 0, 0),
-    ),
-    (),
-    (
-        ("s", 1, 0, 0),
-    ),
-    (),
-    (),
-    (),
-    (
-        ("gv", 1, 0, 2), ("gh", 1, 0, 1),
-    ),
-    (
-        ("s", 1, 0, 3),
-    ),
-    (
-        ("s", 0, 1, 0),
-    ),
-    (),
-    (
-        ("v", 0, 1, 0), ("gh", 1, 1, 0),
-    ),
-    (
-        ("s", 0, 1, 3), ("v", 0, 1, 3), ("h", 0, 1, 3), ("s", 0, 1, 1), ("f", 0, 0, 0), ("v", 0, 1, 1),
-        ("h", 0, 1, 0),
-    ),
-    (
-        ("f", 0, 0, 1), ("s", 0, 1, 2), ("v", 0, 1, 2), ("h", 0, 1, 2),
-    ),
-    (
-        ("s", 1, 1, 3), ("s", 1, 0, 1), ("gv", 1, 1, 3), ("h", 0, 1, 1), ("s", 1, 1, 0),
-    ),
-    (
-        ("f", 0, 1, 0), ("v", 1, 1, 0), ("gh", 1, 1, 1), ("s", 1, 1, 2), ("v", 0, 0, 3), ("gh", 1, 1, 2),
-    ),
-    (
-        ("s", 1, 1, 1), ("f", 0, 0, 2), ("v", 1, 0, 0),
-    ),
-    (
-        ("gh", 1, 0, 3), ("f", 0, 1, 1), ("v", 0, 0, 0),
-    ),
-    (),
-    (),
-    (),
-    (
-        ("f", 0, 0, 3), ("s", 1, 0, 2), ("f", 0, 1, 2),
-    ),
-    (
-        ("f", 0, 1, 3),
+        ("cot", 0, 0, 0), ("s", 0, 0, 3), ("v", 0, 0, 2), ("h", 0, 0, 1), ("s", 0, 0, 2), ("s", 0, 0, 0),
+    ),
+    (),
+    (),
+    (),
+    (),
+    (),
+    (
+        ("gh", 1, 0, 0), ("v", 0, 0, 3),
+    ),
+    (
+        ("s", 0, 0, 1),
+    ),
+    (),
+    (
+        ("s", 1, 0, 1), ("gv", 1, 0, 2), ("h", 0, 0, 2),
+    ),
+    (),
+    (),
+    (),
+    (),
+    (),
+    (
+        ("gv", 1, 1, 1), ("s", 0, 1, 3),
+    ),
+    (
+        ("gh", 1, 1, 0),
+    ),
+    (
+        ("s", 1, 0, 2),
+    ),
+    (
+        ("v", 0, 1, 3), ("s", 0, 1, 2), ("gh", 1, 0, 1), ("v", 0, 0, 0), ("gh", 1, 1, 2), ("s", 0, 1, 0),
+        ("f", 0, 0, 1), ("v", 0, 1, 0), ("h", 0, 1, 2), ("f", 0, 1, 2), ("s", 0, 1, 1), ("h", 0, 1, 1),
+        ("v", 0, 1, 2), ("f", 0, 1, 0), ("s", 1, 1, 2), ("f", 0, 0, 0), ("v", 0, 1, 1), ("h", 0, 1, 0),
+    ),
+    (),
+    (),
+    (
+        ("s", 1, 1, 1), ("v", 1, 1, 1), ("h", 0, 0, 3), ("f", 0, 1, 1), ("s", 1, 1, 0), ("s", 1, 1, 3),
+    ),
+    (
+        ("gh", 1, 0, 3), ("v", 0, 0, 1),
+    ),
+    (
+        ("s", 1, 0, 3), ("s", 1, 0, 0), ("v", 1, 0, 3), ("gh", 1, 1, 3),
+    ),
+    (),
+    (),
+    (),
+    (),
+    (
+        ("f", 0, 0, 3), ("f", 0, 1, 3), ("f", 0, 0, 2),
     ),
     (),
     (),
@@ -109,59 +100,61 @@
         ("gh", 1, 0, 0),
     ),
     (
-        ("gh", 1, 0, 1),
-    ),
-    (
-        ("z", 0, 1, 0),
-    ),
-    (
-        ("gv", 0, 0, 3), ("z", 0, 1, 3), ("gv", 1, 0, 3),
-    ),
-    (),
-    (),
-    (),
-    (
-        ("h", 0, 0, 1), ("s", 0, 0, 1),
-    ),
-    (
-        ("gv", 0, 0, 0),
-    ),
-    (
-        ("z", 0, 1, 1),
-    ),
-    (),
-    (
-        ("gh", 1, 1, 0), ("s", 0, 0, 2), ("z", 0, 1, 2), ("gv", 0, 0, 1),
-    ),
-    (
-        ("h", 0, 0, 2), ("s", 1, 0, 1), ("v", 1, 0, 1), ("gh", 1, 0, 2), ("s", 0, 1, 0), ("gv", 0, 1, 0),
-        ("gh", 1, 1, 1), ("s", 0, 1, 3), ("s", 1, 0, 2), ("gv", 1, 1, 2), ("h", 0, 1, 3), ("s", 0, 1, 1),
-        ("gv", 0, 0, 2), ("h", 0, 1, 1), ("s", 0, 1, 2),
-    ),
-    (
-        ("gv", 0, 1, 1),
-    ),
-    (),
-    (
-        ("h", 0, 1, 2), ("s", 1, 1, 3), ("v", 1, 0, 2), ("gh", 1, 1, 3), ("f", 0, 1, 0), ("s", 1, 1, 0),
-        ("s", 1, 1, 1), ("gv", 0, 1, 2), ("h", 0, 0, 3), ("s", 0, 0, 3),
+        ("gv", 0, 0, 1),
+    ),
+    (
+        ("z", 0, 1, 3),
+    ),
+    (
+        ("s", 0, 0, 2), ("h", 0, 0, 2),
+    ),
+    (),
+    (),
+    (),
+    (
+        ("gv", 1, 0, 1), ("z", 0, 1, 2), ("s", 0, 0, 3),
+    ),
+    (),
+    (
+        ("gh", 1, 1, 0),
+    ),
+    (
+        ("gv", 1, 1, 2),
+    ),
+    (
+        ("z", 0, 1, 0), ("s", 1, 0, 2), ("gh", 1, 1, 3),
+    ),
+    (
+        ("gv", 0, 1, 2), ("gh", 1, 1, 1), ("gv", 0, 1, 0), ("z", 0, 1, 1), ("s", 0, 1, 3), ("h", 0, 1, 3),
+        ("gv", 0, 0, 0), ("s", 0, 0, 0), ("h", 0, 0, 0), ("gv", 0, 1, 1), ("s", 1, 1, 3), ("s", 0, 1, 0),
+        ("h", 0, 1, 0),
+    ),
+    (
+        ("v", 1, 1, 3), ("f", 0, 1, 2), ("s", 1, 0, 0), ("s", 0, 1, 2), ("h", 0, 1, 2), ("v", 1, 0, 0),
+        ("f", 0, 1, 0), ("s", 1, 1, 0),
+    ),
+    (
+        ("s", 0, 1, 1), ("gh", 1, 0, 3), ("gv", 0, 1, 3),
     ),
     (
         ("s", 1, 1, 2),
     ),
     (
-        ("s", 1, 0, 0), ("gv", 0, 1, 3),
-    ),
-    (
-        ("f", 0, 1, 1),
-    ),
-    (
-        ("s", 0, 0, 0), ("s", 1, 0, 3),
-    ),
-    (),
-    (),
-    (
-        ("f", 0, 1, 2), ("f", 0, 1, 3),
+        ("s", 1, 1, 1), ("gh", 1, 0, 2), ("f", 0, 1, 1),
+    ),
+    (
+        ("gv", 0, 0, 3), ("s", 0, 0, 1), ("h", 0, 0, 1),
+    ),
+    (),
+    (),
+    (
+        ("gv", 0, 0, 2), ("s", 1, 0, 3),
+    ),
+    (
+        ("s", 1, 0, 1),
+    ),
+    (
+        ("f", 0, 1, 3),
     ),
     (),
     (),
@@ -577,12 +570,14 @@
 def deliver(*refs):
     sem = refs[-1]
     half = len(refs) // 2
-    pairs = list(zip(refs[:half], refs[half:-1]))
-    ig, ig_out = pairs.pop(1)
+    small = list(zip(refs[:half], refs[half:-1]))
+    ig, ig_out = small.pop(1)
     quarter = TOK // 4
+    pairs = []
     for n in range(4):
         rows = pl.ds(n * quarter, quarter)
         pairs.append((ig.at[rows], ig_out.at[rows]))
+    pairs += small
     copies = [pltpu.make_async_copy(a, b, sem.at[i]) for i, (a, b) in enumerate(pairs)]
     for copy in copies:
         copy.start()

time: 55.4 us -> 55.5 us (level)
  no operation moved by 1% of the time
where the time goes in v5:
time: 55.5 us; the launch traced here: 54.6 us
  Pallas kernels  53.3 us (96%)
  between operations  1.29 us (2%)
    pallas_call x1, Pallas kernels, local(): pl.pallas_call(kernel, out_shape=(jax.ShapeDtypeStruct((TOK, COLS), BF16)...  51 us
    pallas_call x1, Pallas kernels, local(): pl.pallas_call(deliver, out_shape=tuple((jax.ShapeDtypeStruct(o.shape, o....  2.32 us

profile of v5, /device:TPU:32, one launch (start us, length us, event | category | flops | bytes accessed | tf_op | source)
XLA Modules:
  0.0 54.6 jit_solution(2830295687644379357)
XLA Ops:
  1.3 51.0 %shard_map.127 = (bf16[384,256]{1,0:T(8,128)(2,1)S(1)}, bf16[384,4096]{1,0:T(8,128)(2,1)S(1)}, bf16[4,256,256]{2,1,0:T(8,128)(2,1)S(1)}, f32[4,64,256]{2,1,0:T(8...) custom-call(bf16[384,4096]{1,0:T(8,128)(2,1)} %acts_hbm.1, bf16[1024,256]{1,0:T(8,128)(2,1)} %bitcast.8, ...), custom_call_target="tpu_custom_call" | custom-call | tf_op jit(solution)/shard_map/pallas_call | solution.py:598
  52.3 2.3 %shard_map.128 = (bf16[384,256]{1,0:T(8,128)(2,1)}, bf16[384,4096]{1,0:T(8,128)(2,1)}, bf16[4,256,256]{2,1,0:T(8,128)(2,1)}, f32[4,64,256]{2,1,0:T(8,128)}, f32[...) custom-call(bf16[384,256]{1,0:T(8,128)(2,1)S(1)} %get-tuple-element.18.refs_0_, ...), custom_call_target="tpu_custom_call" | custom-call | tf_op jit(solution)/shard_map/pallas_call | solution.py:645
